TPU v7x, 128 devices: a whole 4x4x4 slice. The times are simulated.
128 devices in a mesh: face: 4 (over y), patch: 32 (over x, z, core).
Axes of the slice: x: 4, y: 4, z: 4, core: 2. Of those that a mesh axis runs over, the one named last changes fastest.
Arguments:
- coarse: bfloat16 [128, 512, 512], P(None, 'patch', 'face'), may hold values from -6 to 6
- w_up: bfloat16 [3, 3, 64, 128], replicated, may hold values from -0.375 to 0.375
- w_mix: bfloat16 [3, 3, 64, 64], replicated, may hold values from -0.25 to 0.25
- w_head: float32 [8, 64], replicated, may hold values from -0.75 to 0.75
- send_index: int32 [4, 128, 4096], P('face', 'patch'), may hold values from 0 to 8191, as said below
- slot_ids: int32 [4, 2097152], P(None, ('face', 'patch')), may hold values from 0 to 16383, as said below
- fractions: float32 [2, 2097152], P(None, ('face', 'patch')), may hold values from 0 to 1
- head_cot: float32 [8, 2097152], P(None, ('face', 'patch')), may hold values from -0.01171875 to 0.01171875
Outputs:
- head: float32 [8, 2097152], P(None, ('face', 'patch'))
- up_grad: float32 [3, 3, 64, 128], replicated
- mix_grad: float32 [3, 3, 64, 64], replicated
- head_grad: float32 [8, 64], replicated
Inputs may be any that keep to these rules, and one draw needn't show every extreme that they name: `send_index`: each row s * 4 + r lists a run of whole consecutive pixel columns of the source, starting at a column boundary, of 2 to 16 columns, its last entry repeated in the slots after the run; for r = 3 the run fills 4096 slots and ends at the block's last pixel, for r = 2 it fills 4096 slots, for smaller r it starts at pixel 0. `slot_ids`: A point's four slots are t, t + 1, t + 256, t + 257 for corners 0..3, all within one run of live slots of one r, and t not in a run's last row.
All inputs are finite; a program needn't handle non-finite values.
Results may differ from a plain program's by a relative error of at most 0.0047.
Values may be sent and summed in bfloat16 or wider, within the bound.
A program may use at most 128 MiB of HBM per device.

v0:
```python
import jax
import jax.numpy as jnp
from jax import lax
from jax.sharding import PartitionSpec as P

PAIRS = (((1, 0),), ((2, 0), (0, 1)))


def extended_2(block, sides, width):
    for axis, dim in sides:
        count = lax.axis_size(axis)
        forward = [(i, i + 1) for i in range(count - 1)]
        forward.append((count - 1, 0))
        backward = [(target, source) for source, target in forward]
        low = lax.ppermute(
            lax.slice_in_dim(block, block.shape[dim] - width, None, axis=dim), axis, forward
        )
        high = lax.ppermute(lax.slice_in_dim(block, 0, width, axis=dim), axis, backward)
        block = jnp.concatenate([low, block, high], axis=dim)
    return block


def shifted(value, axis, steps):
    count = lax.axis_size(axis)
    first, last = (max(0, -steps), min(count, count - steps))
    return lax.ppermute(value, axis, [(source, source + steps) for source in range(first, last)])


def passed_along(value, axis, steps):
    count = lax.axis_size(axis)
    pairs = [(source, (source + steps) % count) for source in range(count)]
    return lax.ppermute(value, axis, pairs)


def matmul_taps(weight, window):
    channels = window.shape[0]
    flat = window.reshape(channels, -1)
    result = jnp.dot(weight, flat, preferred_element_type=jnp.float32)
    return result.reshape((weight.shape[0],) + window.shape[1:])


def tap_grad(grad_window, window):
    left = grad_window.reshape(grad_window.shape[0], -1)
    right = window.reshape(window.shape[0], -1)
    return lax.dot_general(
        left, right, (((1,), (1,)), ((), ())), preferred_element_type=jnp.float32
    )


def up_convolve(extended, w_up):
    narrow = extended.shape[1] - 1
    short = extended.shape[2] - 1
    outer = w_up.shape[2]
    columns = []
    for col_parity in range(2):
        row_parts = []
        for row_parity in range(2):
            summed = jnp.zeros((outer, narrow, short), jnp.float32)
            for col_tap, col_shift in PAIRS[col_parity]:
                for row_tap, row_shift in PAIRS[row_parity]:
                    window = extended[
                        :, col_shift : col_shift + narrow, row_shift : row_shift + short
                    ]
                    summed = summed + matmul_taps(w_up[col_tap, row_tap], window)
            row_parts.append(summed)
        columns.append(jnp.stack(row_parts, axis=3).reshape(outer, narrow, 2 * short))
    return jnp.stack(columns, axis=2).reshape(outer, 2 * narrow, 2 * short)


def up_weight_grad(grad_fine, extended):
    outer = grad_fine.shape[0]
    narrow = extended.shape[1] - 1
    short = extended.shape[2] - 1
    split = grad_fine.reshape(outer, narrow, 2, short, 2)
    table = [[None, None, None] for number in range(3)]
    for col_parity in range(2):
        for row_parity in range(2):
            parity_part = split[:, :, col_parity, :, row_parity]
            for col_tap, col_shift in PAIRS[col_parity]:
                for row_tap, row_shift in PAIRS[row_parity]:
                    window = extended[
                        :, col_shift : col_shift + narrow, row_shift : row_shift + short
                    ]
                    table[col_tap][row_tap] = tap_grad(parity_part, window)
    return jnp.stack([jnp.stack(table[number], axis=0) for number in range(3)], axis=0)


def convolve(padded, weight):
    wide = padded.shape[1] - 2
    tall = padded.shape[2] - 2
    summed = jnp.zeros((weight.shape[2], wide, tall), jnp.float32)
    for col_tap in range(3):
        for row_tap in range(3):
            window = padded[:, col_tap : col_tap + wide, row_tap : row_tap + tall]
            summed = summed + matmul_taps(weight[col_tap, row_tap], window)
    return summed


def convolve_back(padded, weight):
    wide = padded.shape[1] - 2
    tall = padded.shape[2] - 2
    summed = jnp.zeros((weight.shape[3], wide, tall), jnp.float32)
    for col_tap in range(3):
        for row_tap in range(3):
            window = padded[:, 2 - col_tap : 2 - col_tap + wide, 2 - row_tap : 2 - row_tap + tall]
            summed = summed + matmul_taps(weight[col_tap, row_tap].T, window)
    return summed


def conv_weight_grad(grad_out, padded):
    wide = padded.shape[1] - 2
    tall = padded.shape[2] - 2
    table = []
    for col_tap in range(3):
        line = []
        for row_tap in range(3):
            line.append(
                tap_grad(grad_out, padded[:, col_tap : col_tap + wide, row_tap : row_tap + tall])
            )
        table.append(jnp.stack(line, axis=0))
    return jnp.stack(table, axis=0)


def swish(value):
    return value * jax.nn.sigmoid(value)


def swish_slope(value):
    sigma = jax.nn.sigmoid(value)
    return sigma * (1.0 + value * (1.0 - sigma))


def bilinear(fractions):
    along = fractions[0]
    across = fractions[1]
    return jnp.stack(
        [
            (1.0 - along) * (1.0 - across),
            along * (1.0 - across),
            (1.0 - along) * across,
            along * across,
        ],
        axis=0,
    )


def corner_table(values, stride):
    count = values.shape[0]
    width = values.shape[1]
    extra = jnp.zeros((stride + 1, width), values.dtype)
    longer = jnp.concatenate([values, extra], axis=0)
    return jnp.concatenate(
        [
            longer[:count],
            longer[1 : count + 1],
            longer[stride : count + stride],
            longer[stride + 1 : count + stride + 1],
        ],
        axis=1,
    )


def interpolate(values, slot_ids, weights, stride):
    rows_major = values.T
    width = rows_major.shape[1]
    table = corner_table(rows_major, stride)
    picked = jnp.take(table, slot_ids[0], axis=0).reshape(-1, 4, width)
    summed = weights[0][:, None] * picked[:, 0].astype(jnp.float32)
    for corner in range(1, 4):
        summed = summed + weights[corner][:, None] * picked[:, corner].astype(jnp.float32)
    return summed.T


def shifted_down(value, amount):
    count = value.shape[0]
    head_rows = jnp.zeros((amount, value.shape[1]), value.dtype)
    return jnp.concatenate([head_rows, value[: count - amount]], axis=0)


def spread(values, slot_ids, weights, count, stride):
    width = values.shape[0]
    cols = values.T
    terms = jnp.concatenate([weights[corner][:, None] * cols for corner in range(4)], axis=1)
    gathered = jnp.zeros((count, 4 * width), jnp.float32).at[slot_ids[0]].add(terms)
    parts = gathered.reshape(count, 4, width)
    summed = parts[:, 0] + shifted_down(parts[:, 1], 1)
    summed = summed + shifted_down(parts[:, 2], stride) + shifted_down(parts[:, 3], stride + 1)
    return summed.T


def inner_rows(left, right):
    return lax.dot_general(
        left,
        right,
        (((1,), (1,)), ((), ())),
        precision=lax.Precision.HIGHEST,
        preferred_element_type=jnp.float32,
    )


def fine_rim(value):
    padded = extended_2(value, (("face", 2), ("patch", 1)), 1)
    position = lax.axis_index("face")
    top_face = lax.axis_size("face") - 1
    height = padded.shape[2]
    row_index = lax.broadcasted_iota(jnp.int32, (1, 1, height), 2)
    inside = jnp.logical_and(
        jnp.logical_or(row_index > 0, position > 0),
        jnp.logical_or(row_index < height - 1, position < top_face),
    )
    return jnp.where(inside, padded, jnp.zeros_like(padded))


def select_runs(flat, starts, reach, capacity):
    pieces = [
        lax.dynamic_slice_in_dim(flat, starts[number], capacity, 1) for number in range(reach)
    ]
    return jnp.concatenate(pieces, axis=1)


def place_runs(values, starts, reach, capacity, pixel_count):
    total = jnp.zeros((values.shape[0], pixel_count), jnp.float32)
    for number in range(reach):
        piece = values[:, number * capacity : (number + 1) * capacity]
        current = lax.dynamic_slice_in_dim(total, starts[number], capacity, 1)
        total = lax.dynamic_update_slice_in_dim(total, current + piece, starts[number], 1)
    return total


def route(values, reach, mover):
    channels = values.shape[0]
    blocks = values.reshape(channels, reach, -1)
    pieces = []
    for number in range(reach):
        offset = reach - 2 - number
        piece = blocks[:, number]
        if offset != 0:
            piece = mover(piece, offset)
        pieces.append(piece)
    return jnp.stack(pieces, axis=1).reshape(channels, -1)


def per_device(coarse, w_up, w_mix, w_head, send_index, slot_ids, fractions, head_cot):
    row_next = shifted(coarse[:, :, :1], "face", -1)
    taller = jnp.concatenate([coarse, row_next], axis=2)
    col_next = passed_along(taller[:, :1, :], "patch", -1)
    extended = jnp.concatenate([taller, col_next], axis=1)
    first = up_convolve(extended, w_up)
    hidden = swish(first).astype(jnp.bfloat16)
    hidden_pad = fine_rim(hidden)
    second = convolve(hidden_pad, w_mix)
    features = swish(second).astype(jnp.bfloat16)
    channels = features.shape[0]
    stride = features.shape[2]
    flat_feat = features.reshape(channels, -1)
    pixel_count = flat_feat.shape[1]
    reach = send_index.shape[1]
    capacity = send_index.shape[2]
    starts = send_index[0, :, 0]
    slot_count = reach * capacity
    weights = bilinear(fractions)
    outgoing = select_runs(flat_feat, starts, reach, capacity)
    arrived = route(outgoing, reach, lambda piece, offset: passed_along(piece, "patch", -offset))
    sampled = interpolate(arrived, slot_ids, weights, stride)
    head = jnp.dot(w_head, sampled, precision=lax.Precision.HIGHEST)
    head_grad = inner_rows(head_cot, sampled)
    feat_cot = jnp.dot(w_head.T, head_cot, precision=lax.Precision.HIGHEST)
    slot_cot = spread(feat_cot, slot_ids, weights, slot_count, stride)
    returned = route(slot_cot, reach, lambda piece, offset: passed_along(piece, "patch", offset))
    pixel_cot = place_runs(returned, starts, reach, capacity, pixel_count)
    fine_cot = pixel_cot.reshape(features.shape)
    second_cot = (fine_cot * swish_slope(second)).astype(jnp.bfloat16)
    mix_grad = conv_weight_grad(second_cot, hidden_pad)
    hidden_cot = convolve_back(fine_rim(second_cot), w_mix)
    first_cot = (hidden_cot * swish_slope(first)).astype(jnp.bfloat16)
    up_grad = up_weight_grad(first_cot, extended)
    up_grad, mix_grad, head_grad = lax.psum((up_grad, mix_grad, head_grad), ("face", "patch"))
    return (head, up_grad, mix_grad, head_grad)


def solution(mesh):
    placed = (
        P(None, "patch", "face"),
        P(),
        P(),
        P(),
        P("face", "patch", None),
        P(None, ("face", "patch")),
        P(None, ("face", "patch")),
        P(None, ("face", "patch")),
    )
    return jax.shard_map(
        per_device,
        mesh=mesh,
        in_specs=placed,
        out_specs=(P(None, ("face", "patch")), P(), P(), P()),
        check_vma=False,
    )
```

profile of v0, /device:TPU:1, one launch (start us, length us, event | category | flops | bytes accessed | tf_op | source)
XLA Modules:
  0.0 657.2 jit_solution(870240383344295814)
XLA Ops:
  8.4 5.2 broadcast_multiply_fusion.3
  13.7 6.2 pad_maximum_fusion
  19.9 17.5 %copy.147 = f32[16384,256]{1,0:T(8,128)} copy(f32[16384,256]{0,1:T(8,128)} %pad_maximum_fusion) | data formatting | bytes 33554432 | tf_op jit(solution)/shard_map/concatenate | solution.py:183
  37.4 95.0 %scatter_custom_fusion = f32[16384,256]{1,0:T(8,128)} fusion(s32[16384]{0:T(1024)S(1)} %bitcast.544, f32[16384,256]{1,0:T(8,128)} %copy.147, f32[]{:T(128)} %constant.23.clone.1), kind=kCustom, calls=%fused_computation.22 | custom fusion | flops 4194304 | bytes 16777728 | tf_op jit(solution)/shard_map/scatter-add | solution.py:184
  132.5 17.4 %copy.148 = f32[16384,256]{0,1:T(8,128)} copy(f32[16384,256]{1,0:T(8,128)} %scatter_custom_fusion) | data formatting | bytes 33554432 | tf_op jit(solution)/shard_map/scatter-add | solution.py:184
  149.9 2.5 slice_bitcast_fusion
  152.4 2.4 slice_bitcast_fusion.2
  154.9 2.4 slice_bitcast_fusion.3
  157.3 6.4 fusion.6
  163.7 6.0 reshape.345
  169.7 11.7 %fusion.129 = (f32[64,1,4096]{2,1,0:T(1,128)S(1)}, f32[64,1,4096]{2,1,0:T(1,128)S(1)}, f32[64,1,4096]{2,1,0:T(1,128)}, f32[64,1,4096]{2,1,0:T(1,128)}) fusion(f32[64,4,4096]{2,1,0:T(4,128)} %reshape.345), kind=kLoop, calls=%fused_computation.271 | loop fusion | bytes 8388608 | tf_op jit(solution)/shard_map/slice | solution.py:236
  182.9 2.5 collective-permute-start.9
  185.4 1.7 copy.276
  187.1 2.5 collective-permute-start.10
  192.0 2.8 collective-permute-done
  196.3 2.5 collective-permute-done.1
  200.7 2.3 fusion.125
  202.9 3.1 copy.125
  206.0 4.1 copy.130
  210.1 3.8 pad_maximum_fusion.2
  213.9 3.8 copy.131
  217.7 2.1 fusion.23
  225.1 9.3 %collective-permute-done.2 = bf16[64,32,1]{2,0,1:T(8,128)(2,1)S(1)} collective-permute-done((bf16[64,32,1]{2,0,1:T(8,128)(2,1)}, bf16[64,32,1]{2,0,1:T(8,128)(2,1)S(1)}, u32[]{:S(2)}, u32[]{:S(2)}) %collective-permute-start.2) | collective-permute-done | bytes 4128 | tf_op jit(solution)/shard_map/ppermute | solution.py:15
  234.5 1.8 collective-permute-start.4
  245.1 2.4 maximum_select_fusion
  247.4 2.4 slice_bitcast_fusion.17
  254.6 2.1 fusion.24
  259.1 4.5 reshape.342
  263.6 8.7 %fusion.130 = (bf16[64,1,4096]{2,1,0:T(2,128)(2,1)S(1)}, bf16[64,1,4096]{2,1,0:T(2,128)(2,1)S(1)}, bf16[64,1,4096]{2,1,0:T(2,128)(2,1)S(1)}, bf16[64,1,4096]{2,1,0:T(2,128)(2,1)S(1)}) fusion(bf16[64,4,4096]{2,1,0:T(4,128)(2,1)} %reshape.342), kind=kLoop, calls=%fused_computation.272 | loop fusion | bytes 4194304 | tf_op jit(solution)/shard_map/slice | solution.py:236
  272.9 4.7 collective-permute-start.6
  279.2 1.7 collective-permute-start.8
  284.3 4.4 collective-permute-done.6
  289.8 2.4 collective-permute-done.7
  292.2 1.6 pad_maximum_fusion.4
  293.8 4.8 copy.145
  298.6 8.3 %pad_slice_fusion.2 = (bf16[16384,64]{1,0:T(8,128)(2,1)S(1)}, bf16[16384,64]{1,0:T(8,128)(2,1)S(1)}, bf16[16384,64]{1,0:T(8,128)(2,1)S(1)}) fusion(bf16[16384,64]{1,0:T(8,128)(2,1)} %bitcast.478), kind=kLoop, calls=%fused_computation.44 | loop fusion | bytes 8388608 | tf_op jit(solution)/shard_map/slice | solution.py:155
  307.0 7.3 %pad_maximum_fusion.1 = bf16[16384,256]{1,0:T(8,128)(2,1)} fusion(bf16[16384,64]{1,0:T(8,128)(2,1)S(1)} %get-tuple-element.16, bf16[16384,64]{1,0:T(8,128)(2,1)S(1)} %get-tuple-element.15, bf16[16384,64]{1,0:T(8,128)(2,1)S(1)} %get-tuple-element.14, bf16[16384,64]{1,0:T(8,128)(2,1)S(1)} %bitcast.479), kind=kLoop, calls=%fused_computation.21 | loop fusion | flops 33554432 | bytes 16777216 | tf_op jit(solution)/shard_map/concatenate | solution.py:152
  314.3 70.5 %gather_fusion = bf16[16384,256]{1,0:T(8,128)(2,1)} fusion(bf16[16384,256]{1,0:T(8,128)(2,1)} %pad_maximum_fusion.1, s32[16384]{0:T(1024)} %broadcast_clamp_fusion), kind=kCustom, calls=%fused_computation | custom fusion | bytes 16842752 | tf_op jit(solution)/shard_map/jit(_take)/gather | solution.py:167
  384.8 12.0 %copy.146 = bf16[16384,256]{0,1:T(8,128)(2,1)} copy(bf16[16384,256]{1,0:T(8,128)(2,1)} %gather_fusion) | data formatting | bytes 16777216 | tf_op jit(solution)/shard_map/jit(_take)/gather | solution.py:167
  396.8 7.8 %broadcast_select_fusion = bf16[16384,4,64]{0,2,1:T(8,128)(2,1)} fusion(bf16[16384,4,64]{0,2,1:T(8,128)(2,1)} %bitcast.480, pred[16384]{0:T(1024)(128)(4,1)S(1)} %compare_and_fusion), kind=kLoop, calls=%fused_computation.24 | loop fusion | flops 4194304 | bytes 16793600 | tf_op jit(solution)/shard_map/jit(_take)/select_n | solution.py:167
  404.6 6.9 %convolution_bitcast_fusion.25 = f32[8,64]{1,0:T(8,128)S(1)} fusion(f32[8,16384]{1,0:T(8,128)S(1)} %copy-done, bf16[16384,4,64]{0,2,1:T(8,128)(2,1)} %broadcast_select_fusion, f32[16384]{0:T(1024)S(1)} %copy-done.17, f32[16384]{0:T(1024)S(1)} %copy-done.20, f32[16384]{0:T(1024)S(1)} %get-tuple-element.62, f32[16384]{0:T(1024)S(1)} %get-tuple-element.61), kind=kOutput, calls=%fused_computation.112 | convolution fusion | flops 112197632 | bytes 9177088 | tf_op jit(solution)/shard_map/dot_general | solution.py:192
  411.6 2.2 maximum_bitcast_fusion
  414.2 2.0 copy-done.2
  417.8 5.8 dynamic_update_slice.12
  423.6 1.9 slice_add_fusion.2
  425.5 5.8 dynamic_update_slice.13
  431.2 1.9 slice_add_fusion.1
  433.1 5.6 dynamic_update_slice.14
  438.7 1.9 slice_add_fusion
  440.6 5.2 dynamic_update_slice.15
  445.8 2.9 fusion.16
  454.9 1.6 collective-permute-start.13
  456.5 8.7 %collective-permute-done.12 = bf16[64,32,1]{2,0,1:T(8,128)(2,1)S(1)} collective-permute-done((bf16[64,32,1]{2,0,1:T(8,128)(2,1)S(1)}, bf16[64,32,1]{2,0,1:T(8,128)(2,1)S(1)}, u32[]{:S(2)}, u32[]{:S(2)}) %collective-permute-start.12) | collective-permute-done | bytes 4128 | tf_op jit(solution)/shard_map/ppermute | solution.py:15
  465.3 3.9 collective-permute-start.14
  470.4 2.3 collective-permute-done.15
  474.0 2.4 slice_bitcast_fusion.8
  481.5 2.8 copy.165
  484.3 5.5 copy.166
  489.8 2.3 multiply_convert_fusion
  497.0 8.0 %convolution_bitcast_fusion = f32[8,16384]{1,0:T(8,128)} fusion(f32[8,64]{1,0:T(8,128)S(1)} %copy-done.26, bf16[16384,4,64]{0,2,1:T(8,128)(2,1)} %broadcast_select_fusion, f32[16384]{0:T(1024)S(1)} %copy-done.18, f32[16384]{0:T(1024)S(1)} %copy-done.21, f32[16384]{0:T(1024)S(1)} %get-tuple-element.62, f32[16384]{0:T(1024)S(1)} %get-tuple-element.61), kind=kOutput, calls=%fused_computation.2 | convolution fusion | flops 112197632 | bytes 9177088 | tf_op jit(solution)/shard_map/dot_general | solution.py:265
  505.0 70.7 %psum.23 = f32[8,64]{1,0:T(8,128)} all-reduce(f32[8,64]{1,0:T(8,128)S(1)} %convolution_bitcast_fusion.25), channel_id=1, replica_groups=mesh['face'=4,'patch'=32] {'face','patch'}, use_global_device_ids=true, to_apply=%region_3.4 | all-reduce | flops 512 | bytes 4096 | tf_op jit(solution)/shard_map/psum | solution.py:277
  575.7 70.9 %all-reduce.7.cloned.1.call-done = (f32[3,3,64,128]{3,2,1,0:T(8,128)}, f32[3,3,64,64]{3,2,1,0:T(8,128)}) async-done(((f32[3,3,64,128]{3,2,1,0:T(8,128)}, f32[3,3,64,64]{3,2,1,0:T(8,128)}), (f32[3,3,64,128]{3,2,1,0:T(8,128)}, f32[3,3,64,64]{3,2,1,0:T(8,128)})) %all-reduce.7.cloned.1.call-update) | async-done | bytes 442384 | tf_op jit(solution)/shard_map/psum | solution.py:277
  646.6 1.7 copy.289
  648.2 1.7 copy.290
  (182 shorter events, 48.9 us)
Async XLA Ops:
  7.2 1.2 copy-start
  7.2 639.4 %all-reduce.7.cloned.1.call-start = ((), (), s32[]{:S(2)}) async-start(), calls=%async_computation | async-start | bytes 1179648 | tf_op jit(solution)/shard_map/psum | solution.py:277
  8.4 5.3 copy-start.16
  8.4 5.3 copy-start.19
  19.9 17.5 %copy-start.22 = (s32[4,16384]{1,0:T(4,128)S(1)}, s32[4,16384]{1,0:T(4,128)}, u32[]{:S(2)}) copy-start(s32[4,16384]{1,0:T(4,128)} %param.13) | copy-start | bytes 786436
  37.4 95.1 %copy-start.23 = (s32[16384,1]{0,1:T(1,128)}, s32[16384,1]{0,1:T(1,128)S(1)}, u32[]{:S(2)}) copy-start(s32[16384,1]{0,1:T(1,128)S(1)} %compare_select_fusion) | copy-start | bytes 196612
  181.3 8.2 %copy-start.11 = (bf16[128,16,128]{2,1,0:T(8,128)(2,1)S(1)}, bf16[128,16,128]{2,1,0:T(8,128)(2,1)}, u32[]{:S(2)}) copy-start(bf16[128,16,128]{2,1,0:T(8,128)(2,1)} %param.8) | copy-start | bytes 1572868
  182.9 228.6 %collective-permute-start.9 = (f32[64,4096]{1,0:T(8,128)}, f32[64,4096]{1,0:T(8,128)}, u32[]{:S(2)}, u32[]{:S(2)}) collective-permute-start(f32[64,4096]{1,0:T(8,128)} %bitcast.467), channel_id=1, source_target_pairs={{0,2},{1,3},{2,4},{3,5},{4,6},{5,7},{6,8},{7,9},{8,10},{9,11},{10,... | collective-permute-start | bytes 3145736 | tf_op jit(solution)/shard_map/ppermute | solution.py:32
  187.1 4.7 copy-start.25
  187.1 224.5 %collective-permute-start.10 = (f32[64,4096]{1,0:T(8,128)}, f32[64,4096]{1,0:T(8,128)}, u32[]{:S(2)}, u32[]{:S(2)}) collective-permute-start(f32[64,4096]{1,0:T(8,128)} %bitcast.466), channel_id=1, source_target_pairs={{0,1},{1,2},{2,3},{3,4},{4,5},{5,6},{6,7},{7,8},{8,9},{9,10},{10,1... | collective-permute-start | bytes 3145736 | tf_op jit(solution)/shard_map/ppermute | solution.py:32
  190.0 4.8 collective-permute-start
  194.8 4.0 collective-permute-start.1
  195.2 0.8 copy-start.3
  199.1 1.2 copy-start.5
  199.1 1.2 copy-start.7
  220.9 13.4 %collective-permute-start.2 = (bf16[64,32,1]{2,0,1:T(8,128)(2,1)}, bf16[64,32,1]{2,0,1:T(8,128)(2,1)S(1)}, u32[]{:S(2)}, u32[]{:S(2)}) collective-permute-start(bf16[64,32,1]{2,0,1:T(8,128)(2,1)} %get-tuple-element.57), channel_id=1, source_target_pairs={{0,32},{32,64},{64,96},{96,0},{1,33},{33,65},{65,97},{97,1},{2,34}... | collective-permute-start | bytes 12296 | tf_op jit(solution)/shard_map/ppermute | solution.py:15
  222.2 12.1 %collective-permute-start.3 = (bf16[64,32,1]{2,0,1:T(8,128)(2,1)S(1)}, bf16[64,32,1]{2,0,1:T(8,128)(2,1)S(1)}, u32[]{:S(2)}, u32[]{:S(2)}) collective-permute-start(bf16[64,32,1]{2,0,1:T(8,128)(2,1)S(1)} %get-tuple-element.58), channel_id=1, source_target_pairs={{32,0},{64,32},{96,64},{0,96},{33,1},{65,33},{97,65},{1,97},{34,2}... | collective-permute-start | bytes 12296 | tf_op jit(solution)/shard_map/ppermute | solution.py:18
  234.4 10.7 %copy-start.13 = (bf16[64,32,1]{2,0,1:T(8,128)(2,1)}, bf16[64,32,1]{2,0,1:T(8,128)(2,1)S(1)}, u32[]{:S(2)}) copy-start(bf16[64,32,1]{2,0,1:T(8,128)(2,1)S(1)} %collective-permute-done.2) | copy-start | bytes 12292
  234.4 10.7 %copy-start.14 = (bf16[64,32,1]{2,0,1:T(8,128)(2,1)}, bf16[64,32,1]{2,0,1:T(8,128)(2,1)S(1)}, u32[]{:S(2)}) copy-start(bf16[64,32,1]{2,0,1:T(8,128)(2,1)S(1)} %collective-permute-done.3) | copy-start | bytes 12292
  234.5 10.6 %collective-permute-start.4 = (bf16[64,1,258]{2,0,1:T(8,128)(2,1)S(1)}, bf16[64,1,258]{2,0,1:T(8,128)(2,1)S(1)}, u32[]{:S(2)}, u32[]{:S(2)}) collective-permute-start(bf16[64,1,258]{2,0,1:T(8,128)(2,1)S(1)} %get-tuple-element.23), channel_id=1, source_target_pairs={{0,1},{1,2},{2,3},{3,4},{4,5},{5,6},{6,7},{7,8},{8,9},{9,10},{10,1... | collective-permute-start | bytes 99080 | tf_op jit(solution)/shard_map/ppermute | solution.py:15
  236.2 8.8 %collective-permute-start.5 = (bf16[64,1,258]{2,0,1:T(8,128)(2,1)S(1)}, bf16[64,1,258]{2,0,1:T(8,128)(2,1)S(1)}, u32[]{:S(2)}, u32[]{:S(2)}) collective-permute-start(bf16[64,1,258]{2,0,1:T(8,128)(2,1)S(1)} %get-tuple-element.24), channel_id=1, source_target_pairs={{1,0},{2,1},{3,2},{4,3},{5,4},{6,5},{7,6},{8,7},{9,8},{10,9},{11,1... | collective-permute-start | bytes 99080 | tf_op jit(solution)/shard_map/ppermute | solution.py:18
  250.4 0.9 copy-start.15
  272.3 8.6 %slice-start = ((s32[4,16384]{1,0:T(4,128)}), s32[1,16384]{1,0:T(1,128)S(1)}, s32[]{:S(2)}) async-start(s32[4,16384]{1,0:T(4,128)} %param.13), calls=%async_computation.1 | async-start | bytes 131072 | tf_op jit(solution)/shard_map/slice | solution.py:167
  272.3 8.6 %copy-start.10 = (f32[64,1,4096]{2,1,0:T(1,128)S(1)}, f32[64,1,4096]{2,1,0:T(1,128)}, u32[]{:S(2)}) copy-start(f32[64,1,4096]{2,1,0:T(1,128)} %get-tuple-element.8) | copy-start | bytes 3145732
  272.9 15.9 %collective-permute-start.6 = (bf16[64,4096]{1,0:T(8,128)(2,1)S(1)}, bf16[64,4096]{1,0:T(8,128)(2,1)S(1)}, u32[]{:S(2)}, u32[]{:S(2)}) collective-permute-start(bf16[64,4096]{1,0:T(8,128)(2,1)S(1)} %bitcast.537), channel_id=1, source_target_pairs={{0,30},{1,31},{2,0},{3,1},{4,2},{5,3},{6,4},{7,5},{8,6},{9,7},{10,... | collective-permute-start | bytes 1572872 | tf_op jit(solution)/shard_map/ppermute | solution.py:32
  278.1 4.4 copy-start.9
  278.1 14.1 %collective-permute-start.7 = (bf16[64,4096]{1,0:T(8,128)(2,1)S(1)}, bf16[64,4096]{1,0:T(8,128)(2,1)S(1)}, u32[]{:S(2)}, u32[]{:S(2)}) collective-permute-start(bf16[64,4096]{1,0:T(8,128)(2,1)S(1)} %bitcast.536), channel_id=1, source_target_pairs={{0,31},{1,0},{2,1},{3,2},{4,3},{5,4},{6,5},{7,6},{8,7},{9,8},{10,9... | collective-permute-start | bytes 1572872 | tf_op jit(solution)/shard_map/ppermute | solution.py:32
  279.2 13.1 %collective-permute-start.8 = (bf16[64,4096]{1,0:T(8,128)(2,1)S(1)}, bf16[64,4096]{1,0:T(8,128)(2,1)S(1)}, u32[]{:S(2)}, u32[]{:S(2)}) collective-permute-start(bf16[64,4096]{1,0:T(8,128)(2,1)S(1)} %bitcast.538), channel_id=1, source_target_pairs={{0,1},{1,2},{2,3},{3,4},{4,5},{5,6},{6,7},{7,8},{8,9},{9,10},{10,1... | collective-permute-start | bytes 1572872 | tf_op jit(solution)/shard_map/ppermute | solution.py:32
  280.9 2.2 copy-start.24
  288.8 122.8 %collective-permute-start.11 = (f32[64,4096]{1,0:T(8,128)}, f32[64,4096]{1,0:T(8,128)}, u32[]{:S(2)}, u32[]{:S(2)}) collective-permute-start(f32[64,4096]{1,0:T(8,128)} %bitcast.468), channel_id=1, source_target_pairs={{0,31},{1,0},{2,1},{3,2},{4,3},{5,4},{6,5},{7,6},{8,7},{9,8},{10,9... | collective-permute-start | bytes 3145736 | tf_op jit(solution)/shard_map/ppermute | solution.py:32
  298.6 8.4 %copy-start.1 = (bf16[64,4,4096]{0,2,1:T(8,128)(2,1)S(1)}, bf16[64,4,4096]{0,2,1:T(8,128)(2,1)}, u32[]{:S(2)}) copy-start(bf16[64,4,4096]{0,2,1:T(8,128)(2,1)} %copy.145) | copy-start | bytes 6291460
  396.8 7.8 %copy-start.17 = (f32[16384]{0:T(1024)S(1)}, f32[16384]{0:T(1024)}, u32[]{:S(2)}) copy-start(f32[16384]{0:T(1024)} %copy-done.16) | copy-start | bytes 196612
  396.8 7.8 %copy-start.20 = (f32[16384]{0:T(1024)S(1)}, f32[16384]{0:T(1024)}, u32[]{:S(2)}) copy-start(f32[16384]{0:T(1024)} %copy-done.19) | copy-start | bytes 196612
  414.2 2.1 copy-start.2
  453.7 11.5 %collective-permute-start.12 = (bf16[64,32,1]{2,0,1:T(8,128)(2,1)S(1)}, bf16[64,32,1]{2,0,1:T(8,128)(2,1)S(1)}, u32[]{:S(2)}, u32[]{:S(2)}) collective-permute-start(bf16[64,32,1]{2,0,1:T(8,128)(2,1)S(1)} %get-tuple-element.51), channel_id=1, source_target_pairs={{0,32},{32,64},{64,96},{96,0},{1,33},{33,65},{65,97},{97,1},{2,34}... | collective-permute-start | bytes 12296 | tf_op jit(solution)/shard_map/ppermute | solution.py:15
  454.9 10.4 %collective-permute-start.13 = (bf16[64,32,1]{2,0,1:T(8,128)(2,1)S(1)}, bf16[64,32,1]{2,0,1:T(8,128)(2,1)S(1)}, u32[]{:S(2)}, u32[]{:S(2)}) collective-permute-start(bf16[64,32,1]{2,0,1:T(8,128)(2,1)S(1)} %get-tuple-element.52), channel_id=1, source_target_pairs={{32,0},{64,32},{96,64},{0,96},{33,1},{65,33},{97,65},{1,97},{34,2}... | collective-permute-start | bytes 12296 | tf_op jit(solution)/shard_map/ppermute | solution.py:18
  465.3 5.1 collective-permute-start.14
  469.3 3.5 collective-permute-start.15
  492.2 1.0 copy-start.8
  492.2 1.3 copy-start.6
  492.2 1.7 copy-start.4
  492.3 1.8 copy-start.12
  495.3 1.6 copy-start.18
  495.4 1.6 copy-start.21
  495.4 1.6 copy-start.26
Sparse Core Ops, SparseCore 0:
  497.1 149.3 all-reduce.6
where the time goes:
time: 668 us; the launch traced here: 657 us
  local copies, waits for them, and re-layouts  240 us (36%)
  other arithmetic  153 us (23%)
  waiting for transfers between devices  103 us (15%)
  blocking collectives  70.7 us (11%)
  matrix products  39.5 us (6%)
  starting transfers between devices  26.9 us (4%)
  between operations  23.3 us (3%)
    scatter-add x1, other arithmetic, spread(): jnp.zeros((count, 4 * width), jnp.float32).at[slot_ids[0]].add(terms)  95 us
    gather x2, local copies, waits for them, and re-layouts, interpolate(): picked = jnp.take(table, slot_ids[0], axis=0).reshape(-1, 4, width)  82.5 us
    psum x1, waiting for transfers between devices, per_device(): lax.psum((up_grad, mix_grad, head_grad), ('face', 'patch'))  70.9 us
    psum x1, blocking collectives, per_device(): lax.psum((up_grad, mix_grad, head_grad), ('face', 'patch'))  70.7 us
    dynamic_update_slice x4, local copies, waits for them, and re-layouts, place_runs(): lax.dynamic_update_slice_in_dim(total, current + piece, starts[number], 1)  22.4 us
    unnamed x68, local copies, waits for them, and re-layouts  20.3 us
    slice x2, local copies, waits for them, and re-layouts, route(): piece = blocks[:, number]  20.3 us
    ppermute x4, waiting for transfers between devices, extended_2(): lax.ppermute(lax.slice_in_dim(block, block.shape[dim] - width, None, axis...  18.1 us
  transfers between devices with their start and end apart: 17, of which 9 were waited for; matrix products, arithmetic and copies ran while one was open for 28% of the time, Pallas kernels for 0%

commit v1 on v0

v1 whole, which is shorter than its diff:
```python
import functools

import jax
import jax.numpy as jnp
from jax import lax
from jax.experimental import pallas as pl
from jax.experimental.pallas import tpu as pltpu
from jax.sharding import PartitionSpec as P

MESH = pl.DeviceIdType.MESH
F32 = jnp.float32
BF16 = jnp.bfloat16

LANES = 128
CIN = 128
CF = 64
COUT = 8
COLS = 16
POINT_TILE = 512
GRAD_ROWS = 1024
MIX_ROW = 9 * CF
HEAD_ROW = MIX_ROW + 6 * CF
NEIGHBOURS = tuple((df, dp) for df in (-1, 0, 1) for dp in (-1, 0, 1) if (df, dp) != (0, 0))
ROW_NEIGHBOURS = tuple(pair for pair in NEIGHBOURS if pair[0] != 0)


def dot(left, right):
    return lax.dot_general(left, right, (((1,), (0,)), ((), ())), preferred_element_type=F32)


def dot_nt(left, right):
    return lax.dot_general(left, right, (((1,), (1,)), ((), ())), preferred_element_type=F32)


def turn(value, steps):
    if isinstance(steps, int):
        steps = steps % LANES
        if steps == 0:
            return value
    return pltpu.roll(value, steps, axis=1)


def sigmoid(value):
    return 0.5 * jnp.tanh(0.5 * value) + 0.5


def row_weights(slot, along):
    width = slot.shape[1]
    place = lax.broadcasted_iota(jnp.int32, (256, width), 0)
    natural = 2 * (place & 127) + (place >> 7)
    away = natural - (slot & 255)
    weight = jnp.where(away == 0, 1.0 - along, jnp.where(away == 1, along, 0.0))
    return weight.astype(BF16)


def local_kernel(
    nf, npat,
    start_ref, coarse_ref, edge_ref, wup_ref, wmix_ref, wback_ref, whead_ref, wheadt_ref,
    slot_ref, frac_ref, cot_ref,
    head_ref, grad_ref,
    ext, exts, edges, upw, hid, slope1, slope2, feat, gown, gsend, table,
    sacc, srecv, pad, sc, strip, strips, zbuf, fc, mixacc, upacc,
    send_sem, recv_sem,
):
    me_f, me_p = lax.axis_index("face"), lax.axis_index("patch")

    def device(df, dp):
        return (lax.rem(me_f + df + nf, nf), lax.rem(me_p + dp + npat, npat))

    barrier = pltpu.get_barrier_semaphore()
    partners = NEIGHBOURS + ((0, 2), (0, -2))
    for df, dp in partners:
        pl.semaphore_signal(barrier, inc=1, device_id=device(df, dp), device_id_type=MESH)
    pl.semaphore_wait(barrier, len(partners))

    copies = []

    def send(source, target, offset):
        number = len(copies)
        copy = pltpu.make_async_remote_copy(
            src_ref=source, dst_ref=target,
            send_sem=send_sem.at[number], recv_sem=recv_sem.at[number],
            device_id=device(*offset), device_id_type=MESH,
        )
        copy.start()
        copies.append(copy)
        return copy

    coarse_copies = [
        send(coarse_ref.at[0], ext.at[COLS + 1], (0, -1)),
        send(coarse_ref.at[COLS - 1], ext.at[0], (0, 1)),
    ]
    for number, offset in enumerate(NEIGHBOURS):
        coarse_copies.append(send(edge_ref, edges.at[number], offset))

    ext[1 : COLS + 1] = coarse_ref[...]
    ext[COLS + 2] = jnp.zeros((CIN, LANES), BF16)
    for row_tap in range(3):
        low = slice(row_tap * CF, (row_tap + 1) * CF)
        high = slice((3 + row_tap) * CF, (4 + row_tap) * CF)
        upw[low, :CIN] = wup_ref[1, row_tap]
        upw[low, CIN:] = jnp.zeros((CF, CIN), BF16)
        upw[high, :CIN] = wup_ref[2, row_tap]
        upw[high, CIN:] = wup_ref[0, row_tap]

    sacc[...] = jnp.zeros_like(sacc)

    @pl.loop(0, slot_ref.shape[1] // POINT_TILE)
    def _(step):
        here = pl.ds(pl.multiple_of(step * POINT_TILE, POINT_TILE), POINT_TILE)
        slot = slot_ref[0:1, here]
        along, across = frac_ref[0:1, here], frac_ref[1:2, here]
        rows = row_weights(slot, along)
        cot = cot_ref[:, here]
        near, far = cot * (1.0 - across), cot * across
        column = jnp.broadcast_to(slot >> 8, near.shape)[None]
        number = lax.broadcasted_iota(jnp.int32, (64,) + near.shape, 0)
        away = number - column
        terms = jnp.where(away == 0, near[None], jnp.where(away == 1, far[None], 0.0))
        sacc[...] += dot_nt(terms.reshape(64 * COUT, POINT_TILE).astype(BF16), rows)

    run = COLS * COUT
    pad[0:16] = jnp.zeros((16, COUT, 256), F32)
    pad[16:32] = sacc[2 * run : 3 * run].reshape(16, COUT, 256)
    pad[32:48] = jnp.zeros((16, COUT, 256), F32)
    back_copies = [
        send(sacc.at[0:run], srecv.at[0], (0, 2)),
        send(sacc.at[run : 2 * run], srecv.at[1], (0, 1)),
        send(sacc.at[3 * run : 4 * run], srecv.at[2], (0, -1)),
    ]

    for copy in coarse_copies:
        copy.wait_recv()
    lane = lax.broadcasted_iota(jnp.int32, (CIN, LANES), 1)
    lane64 = lane[:CF]
    above = jnp.where(me_f > 0, 1.0, 0.0).astype(F32)
    below = jnp.where(me_f < nf - 1, 1.0, 0.0).astype(F32)

    def arrived(buffer, df, dp):
        pairs = NEIGHBOURS if buffer is edges else ROW_NEIGHBOURS
        return buffer[pairs.index((-df, -dp))].astype(F32)

    def between(low, high, index):
        return jnp.logical_and(index >= low, index < high)

    top = jnp.where(between(1, 17, lane), turn(arrived(edges, -1, 0), -15), 0.0)
    top = jnp.where(lane == 0, turn(arrived(edges, -1, -1), -31), top)
    top = jnp.where(lane == 17, turn(arrived(edges, -1, 1), 1), top) * above
    first_row = jnp.where(between(33, 49, lane), turn(edge_ref[...].astype(F32), 33), 0.0)
    first_row = jnp.where(lane == 32, turn(arrived(edges, 0, -1), 17), first_row)
    first_row = jnp.where(lane == 49, turn(arrived(edges, 0, 1), 49), first_row)
    bottom = jnp.where(between(65, 81, lane), turn(arrived(edges, 1, 0), 65), 0.0)
    bottom = jnp.where(lane == 64, turn(arrived(edges, 1, -1), 49), bottom)
    bottom = jnp.where(lane == 81, turn(arrived(edges, 1, 1), 81), bottom) * below
    rim = top + first_row + bottom
    rim_pair = jnp.concatenate([rim, turn(rim, -1)], axis=0).astype(BF16)
    rim_out = dot(upw[...], rim_pair)
    rim_hidden = []
    for parity in range(2):
        part = rim_out[parity * 192 : (parity + 1) * 192]
        upper = part[128:192] + turn(part[0:64], -32)
        value = jnp.where(lane64 < 32, upper * above, jnp.where(between(64, 96, lane64), part[64:128], 0.0))
        rim_hidden.append(value * sigmoid(value))
    even_rim, odd_rim = rim_hidden
    mix_rim = [
        dot(wmix_ref[...], jnp.concatenate([turn(odd_rim, 1), even_rim, odd_rim], axis=0).astype(BF16)),
        dot(wmix_ref[...], jnp.concatenate([even_rim, odd_rim, turn(even_rim, -1)], axis=0).astype(BF16)),
    ]

    @pl.loop(0, 9)
    def _(step):
        t = 2 * step
        pair = [ext[pl.ds(t + k, 2)].reshape(2 * CIN, LANES) for k in range(2)]
        out = dot(upw[...], jnp.concatenate(pair, axis=1))
        for k in range(2):
            here = t + k
            for parity in range(2):
                part = out[parity * 192 : (parity + 1) * 192, k * LANES : (k + 1) * LANES]
                entering = turn(rim_out[parity * 192 : parity * 192 + 64], 63 - here)
                odd = part[128:192] + jnp.where(lane64 == 127, entering, turn(part[0:64], -1))
                value = jnp.concatenate([part[64:128], odd], axis=1)
                sigma = sigmoid(value)
                hid[2 * here + parity] = (value * sigma).astype(BF16)
                slope1[2 * here + parity] = sigma * (1.0 + value * (1.0 - sigma))
            shifted = turn(ext[here].astype(F32), -1)
            exts[here] = jnp.where(lane == 127, turn(rim, 63 - here), shifted).astype(BF16)

    weight = whead_ref[...]
    weight_high = weight.astype(BF16).astype(F32)
    head_pair = jnp.concatenate([weight_high, weight - weight_high], axis=0).astype(BF16)

    def mix_step(j):
        values = []
        for parity in range(2):
            q = 2 * j + parity
            out = dot(wmix_ref[...], hid[pl.ds(q + 1, 3)].reshape(192, 256))
            low, mid, high = out[0:64], out[64:128], out[128:192]
            first = turn(mix_rim[parity][0:64], 127 - j)
            last = turn(mix_rim[parity][128:192], 62 - j)
            even = jnp.where(lane64 == 0, first, turn(low[:, LANES:], 1)) + mid[:, :LANES] + high[:, LANES:]
            odd = low[:, :LANES] + mid[:, LANES:] + jnp.where(lane64 == 127, last, turn(high[:, :LANES], -1))
            value = jnp.concatenate([even, odd], axis=1)
            sigma = sigmoid(value)
            feature = (value * sigma).astype(BF16)
            feat[q] = feature
            slope2[q] = sigma * (1.0 + value * (1.0 - sigma))
            both = dot(head_pair, feature)
            point_value = both[0:8] + both[8:16]
            gown[q] = point_value
            values.append(point_value)
        gsend[j] = jnp.concatenate(values, axis=0).astype(BF16)

    pl.loop(0, 8)(mix_step)
    value_copies = [
        send(gsend.at[0:8], table.at[0:8], (0, -2)),
        send(gsend.at[0:8], table.at[8:16], (0, -1)),
    ]
    pl.loop(8, 16)(mix_step)
    value_copies.append(send(gsend.at[8:16], table.at[24:32], (0, 1)))

    start = start_ref[0]
    for k in range(8):
        pair = [gown[start + 2 * k], gown[start + 2 * k + 1]]
        table[16 + k] = jnp.concatenate(pair, axis=0).astype(BF16)

    for copy in back_copies:
        copy.wait_recv()
    weight_t = wheadt_ref[...]
    high_t = weight_t.astype(BF16).astype(F32)
    weight_three = jnp.concatenate([high_t, weight_t - high_t, high_t], axis=1).astype(BF16)
    strip[...] = jnp.zeros_like(strip)

    def cot_step(q, total, head_sum):
        high = total.astype(BF16).astype(F32)
        low = total - high
        fine = dot(weight_three, jnp.concatenate([high, high, low], axis=0).astype(BF16))
        value = fine * slope2[q]
        sc[q + 1] = value.astype(BF16)
        kept = jnp.where(lane64 == q, turn(value[:, :LANES], q), strip[...])
        strip[...] = jnp.where(lane64 == q + 32, turn(value[:, LANES:], q + 33), kept)
        both = dot_nt(jnp.concatenate([high, low], axis=0).astype(BF16), feat[q])
        return head_sum + both[0:8] + both[8:16]

    def row_of(number, q):
        return srecv[number, pl.ds(pl.multiple_of(q * COUT, COUT), COUT), :]

    def cot_low(q, head_sum):
        total = row_of(0, q) + row_of(1, q) + pad[16 + q - start]
        return cot_step(q, total, head_sum)

    def cot_high(q, head_sum):
        total = row_of(2, q - 16) + pad[16 + q - start]
        return cot_step(q, total, head_sum)

    head_sum = lax.fori_loop(0, 16, cot_low, jnp.zeros((COUT, CF), F32))
    head_sum = lax.fori_loop(16, 32, cot_high, head_sum)
    strips_own = strips.at[len(ROW_NEIGHBOURS)]
    strips_own[...] = strip[...].astype(BF16)
    cot_copies = [
        send(sc.at[1], sc.at[33], (0, -1)),
        send(sc.at[32], sc.at[0], (0, 1)),
    ]
    for number, offset in enumerate(ROW_NEIGHBOURS):
        cot_copies.append(send(strips_own, strips.at[number], offset))

    for copy in value_copies:
        copy.wait_recv()

    @pl.loop(0, slot_ref.shape[1] // POINT_TILE)
    def _(step):
        here = pl.ds(pl.multiple_of(step * POINT_TILE, POINT_TILE), POINT_TILE)
        slot = slot_ref[0:1, here]
        along, across = frac_ref[0:1, here], frac_ref[1:2, here]
        rows = row_weights(slot, along)
        columns = dot(table[...].reshape(64 * COUT, 256), rows).reshape(64, COUT, POINT_TILE)
        column = jnp.broadcast_to(slot >> 8, (COUT, POINT_TILE))[None]
        number = lax.broadcasted_iota(jnp.int32, (64, COUT, POINT_TILE), 0)
        away = number - column
        near = jnp.broadcast_to(1.0 - across, (COUT, POINT_TILE))[None]
        far = jnp.broadcast_to(across, (COUT, POINT_TILE))[None]
        weights = jnp.where(away == 0, near, jnp.where(away == 1, far, 0.0))
        head_ref[:, here] = jnp.sum(weights * columns, axis=0)

    for copy in cot_copies:
        copy.wait_recv()
    upper = jnp.where(between(1, 33, lane64), turn(arrived(strips, -1, 0), -31), 0.0)
    upper = jnp.where(lane64 == 0, turn(arrived(strips, -1, -1), -63), upper)
    upper = jnp.where(lane64 == 33, turn(arrived(strips, -1, 1), 1), upper) * above
    lower = jnp.where(between(65, 97, lane64), turn(arrived(strips, 1, 0), 65), 0.0)
    lower = jnp.where(lane64 == 64, turn(arrived(strips, 1, -1), 33), lower)
    lower = jnp.where(lane64 == 97, turn(arrived(strips, 1, 1), 97), lower) * below
    cot_rim = upper + lower

    def back_step(w):
        value = sc[w].astype(F32)
        even, odd = value[:, :LANES], value[:, LANES:]
        last = jnp.where(lane64 == 127, turn(cot_rim, 63 - w), turn(even, -1))
        first = jnp.where(lane64 == 0, turn(cot_rim, LANES - w), turn(odd, 1))
        taps = jnp.concatenate(
            [jnp.concatenate([odd, last], axis=1), value, jnp.concatenate([first, even], axis=1)],
            axis=0,
        ).astype(BF16)
        zbuf[w] = dot(wback_ref[...], taps)
        return taps

    mixacc[...] = jnp.zeros_like(mixacc)
    back_step(0)

    @pl.loop(1, 33)
    def _(w):
        taps = back_step(w)
        mixacc[...] += dot_nt(taps, hid[pl.ds(w, 3)].reshape(192, 256))

    back_step(33)

    upacc[...] = jnp.zeros_like(upacc)

    @pl.loop(0, 8)
    def _(step):
        evens, odds = [], []
        for k in range(2):
            even_parts, odd_parts = [], []
            for parity in range(2):
                q = 4 * step + 2 * k + parity
                total = zbuf[q + 2, 0:64] + zbuf[q + 1, 64:128] + zbuf[q, 128:192]
                value = (total * slope1[q + 2]).astype(BF16)
                even_parts.append(value[:, :LANES])
                odd_parts.append(value[:, LANES:])
            evens.append(jnp.concatenate(even_parts, axis=0))
            odds.append(jnp.concatenate(odd_parts, axis=0))
        even = jnp.concatenate(evens, axis=1)
        odd = jnp.concatenate(odds, axis=1)

        def window(buffer):
            pair = [buffer[pl.ds(2 * step + 1 + k, 2)].reshape(2 * CIN, LANES) for k in range(2)]
            return jnp.concatenate(pair, axis=1)

        plain, moved = window(ext), window(exts)
        upacc[0] += dot_nt(odd, moved)
        upacc[1] += dot_nt(even, plain)
        upacc[2] += dot_nt(odd, plain)

    for row_tap in range(3):
        for col_tap, rows, lanes in ((0, 64, 128), (1, 0, 0), (2, 64, 0)):
            at = (col_tap * 3 + row_tap) * CF
            grad_ref[at : at + CF] = upacc[row_tap, rows : rows + CF, lanes : lanes + LANES]
    grad_ref[MIX_ROW : MIX_ROW + 192] = mixacc[:, :LANES]
    grad_ref[MIX_ROW + 192 : HEAD_ROW] = jnp.concatenate(
        [mixacc[:, LANES:], jnp.zeros((192, CF), F32)], axis=1
    )
    grad_ref[HEAD_ROW : HEAD_ROW + COUT] = jnp.concatenate(
        [head_sum, jnp.zeros((COUT, CF), F32)], axis=1
    )
    grad_ref[HEAD_ROW + COUT :] = jnp.zeros((GRAD_ROWS - HEAD_ROW - COUT, LANES), F32)
    for copy in copies:
        copy.wait_send()


def stages_of(nf, npat):
    nz = min(4, max(1, npat // 2))
    nx = npat // (2 * nz)
    return nz, nx


def sum_kernel(nf, npat, grad_ref, up_ref, mix_ref, headg_ref, total, final, one, two, three, send_sem, recv_sem):
    nz, nx = stages_of(nf, npat)
    me_f, me_p = lax.axis_index("face"), lax.axis_index("patch")
    core = lax.rem(me_p, 2)
    z = lax.rem(me_p // 2, nz)
    x = me_p // (2 * nz)

    def core_peer(k):
        return (me_f, me_p - core + lax.rem(core + k, 2))

    def x_peer(k):
        return (me_f, lax.rem(x + k, nx) * 2 * nz + z * 2 + core)

    def zy_peer(k):
        kz, kf = k % nz, k // nz
        return (lax.rem(me_f + kf, nf), x * 2 * nz + lax.rem(z + kz, nz) * 2 + core)

    nzy = nz * nf
    half = GRAD_ROWS // 2
    quarter = half // nx
    piece = quarter // nzy
    groups = ((core_peer, 2), (x_peer, nx), (zy_peer, nzy))

    barrier = pltpu.get_barrier_semaphore()
    count = 0
    for peer, size in groups:
        for k in range(1, size):
            pl.semaphore_signal(barrier, inc=1, device_id=peer(k), device_id_type=MESH)
            count += 1
    pl.semaphore_wait(barrier, count)

    sems = [0]
    pending = []

    def send(source, target, device):
        number = sems[0]
        sems[0] += 1
        copy = pltpu.make_async_remote_copy(
            src_ref=source, dst_ref=target,
            send_sem=send_sem.at[number], recv_sem=recv_sem.at[number],
            device_id=device, device_id_type=MESH,
        )
        copy.start()
        pending.append(copy)
        return copy

    def rows(start, size):
        return pl.ds(pl.multiple_of(start, 8), size)

    def index_core(k):
        return lax.rem(core + k, 2)

    def index_x(k):
        return lax.rem(x + k, nx)

    def index_zy(k):
        return lax.rem(me_f + k // nz, nf) * nz + lax.rem(z + k % nz, nz)

    copy = send(grad_ref.at[rows(index_core(1) * half, half)], one.at[0], core_peer(1))
    copy.wait_recv()
    base = index_core(0) * half
    total[rows(base, half)] = grad_ref[rows(base, half)] + one[0]
    arrivals = [
        send(total.at[rows(base + index_x(k) * quarter, quarter)], two.at[k - 1], x_peer(k))
        for k in range(1, nx)
    ]
    base_x = base + index_x(0) * quarter
    value = total[rows(base_x, quarter)]
    for k, copy in enumerate(arrivals):
        copy.wait_recv()
        value = value + two[k]
    total[rows(base_x, quarter)] = value
    arrivals = [
        send(total.at[rows(base_x + index_zy(k) * piece, piece)], three.at[k - 1], zy_peer(k))
        for k in range(1, nzy)
    ]
    base_zy = base_x + index_zy(0) * piece
    value = total[rows(base_zy, piece)]
    for k, copy in enumerate(arrivals):
        copy.wait_recv()
        value = value + three[k]
    final[rows(base_zy, piece)] = value

    def share(start, size, peer, count):
        region = final.at[rows(start, size)]
        started = [send(region, region, peer(k)) for k in range(1, count)]
        for copy in started:
            copy.wait_recv()

    share(base_zy, piece, zy_peer, nzy)
    share(base_x, quarter, x_peer, nx)
    share(base, half, core_peer, 2)

    up_ref[...] = final[:MIX_ROW]
    for col_tap in range(3):
        for row_tap in range(3):
            at = MIX_ROW + (col_tap // 2) * 192 + row_tap * CF
            lanes = (col_tap % 2) * CF
            to = (col_tap * 3 + row_tap) * CF
            mix_ref[to : to + CF] = final[at : at + CF, lanes : lanes + CF]
    headg_ref[...] = final[HEAD_ROW : HEAD_ROW + COUT, :CF]
    for copy in pending:
        copy.wait_send()


def vmem(count):
    return [pl.BlockSpec(memory_space=pltpu.VMEM)] * count


def per_device(nf, npat, coarse, w_up, w_mix, w_head, send_index, slot_ids, fractions, head_cot):
    by_column = coarse.transpose(1, 0, 2)
    edge = jnp.concatenate(
        [coarse[:, :, 0], coarse[:, :, -1], jnp.zeros((CIN, LANES - 2 * COLS), BF16)], axis=1
    )
    mixing = w_mix.transpose(1, 2, 0, 3).reshape(3 * CF, 3 * CF)
    back = mixing.T
    start = send_index[0, 2, 0:1] // 256
    points = slot_ids.shape[1]
    run = COLS * COUT
    scratch = [
        pltpu.VMEM((COLS + 3, CIN, LANES), BF16),
        pltpu.VMEM((COLS + 2, CIN, LANES), BF16),
        pltpu.VMEM((len(NEIGHBOURS), CIN, LANES), BF16),
        pltpu.VMEM((6 * CF, 2 * CIN), BF16),
        pltpu.VMEM((36, CF, 256), BF16),
        pltpu.VMEM((36, CF, 256), F32),
        pltpu.VMEM((32, CF, 256), F32),
        pltpu.VMEM((32, CF, 256), BF16),
        pltpu.VMEM((32, COUT, 256), F32),
        pltpu.VMEM((16, 16, 256), BF16),
        pltpu.VMEM((32, 16, 256), BF16),
        pltpu.VMEM((4 * run, 256), F32),
        pltpu.VMEM((3, run, 256), F32),
        pltpu.VMEM((48, COUT, 256), F32),
        pltpu.VMEM((34, CF, 256), BF16),
        pltpu.VMEM((CF, LANES), F32),
        pltpu.VMEM((len(ROW_NEIGHBOURS) + 1, CF, LANES), BF16),
        pltpu.VMEM((34, 3 * CF, 256), F32),
        pltpu.VMEM((8, LANES), F32),
        pltpu.VMEM((3 * CF, 3 * CF), F32),
        pltpu.VMEM((3, 2 * CF, 2 * CIN), F32),
        pltpu.SemaphoreType.DMA((24,)),
        pltpu.SemaphoreType.DMA((24,)),
    ]
    head, grads = pl.pallas_call(
        functools.partial(local_kernel, nf, npat),
        out_shape=(
            jax.ShapeDtypeStruct((COUT, points), F32),
            jax.ShapeDtypeStruct((GRAD_ROWS, LANES), F32),
        ),
        in_specs=[pl.BlockSpec(memory_space=pltpu.SMEM)] + vmem(10),
        out_specs=tuple(vmem(2)),
        scratch_shapes=scratch,
        compiler_params=pltpu.CompilerParams(
            collective_id=0, has_side_effects=True, vmem_limit_bytes=56 * 2**20
        ),
        name="local",
    )(start, by_column, edge, w_up, mixing, back, w_head, w_head.T, slot_ids, fractions, head_cot)

    nz, nx = stages_of(nf, npat)
    nzy = nz * nf
    half = GRAD_ROWS // 2
    quarter = half // nx
    piece = quarter // nzy
    sends = 2 * (1 + nx - 1 + nzy - 1)
    up, mix, head_grad = pl.pallas_call(
        functools.partial(sum_kernel, nf, npat),
        out_shape=(
            jax.ShapeDtypeStruct((9 * CF, CIN), F32),
            jax.ShapeDtypeStruct((9 * CF, CF), F32),
            jax.ShapeDtypeStruct((COUT, CF), F32),
        ),
        in_specs=vmem(1),
        out_specs=tuple(vmem(3)),
        scratch_shapes=[
            pltpu.VMEM((GRAD_ROWS, LANES), F32),
            pltpu.VMEM((GRAD_ROWS, LANES), F32),
            pltpu.VMEM((1, half, LANES), F32),
            pltpu.VMEM((max(1, nx - 1), quarter, LANES), F32),
            pltpu.VMEM((nzy - 1, piece, LANES), F32),
            pltpu.SemaphoreType.DMA((sends,)),
            pltpu.SemaphoreType.DMA((sends,)),
        ],
        compiler_params=pltpu.CompilerParams(
            collective_id=1, has_side_effects=True, vmem_limit_bytes=32 * 2**20
        ),
        name="sum",
    )(grads)
    return head, up.reshape(3, 3, CF, CIN), mix.reshape(3, 3, CF, CF), head_grad


def solution(mesh):
    placed = (
        P(None, "patch", "face"),
        P(),
        P(),
        P(),
        P("face", "patch", None),
        P(None, ("face", "patch")),
        P(None, ("face", "patch")),
        P(None, ("face", "patch")),
    )
    return jax.shard_map(
        functools.partial(per_device, mesh.shape["face"], mesh.shape["patch"]),
        mesh=mesh,
        in_specs=placed,
        out_specs=(P(None, ("face", "patch")), P(), P(), P()),
        check_vma=False,
    )
```

time: 668 us -> 113 us (0.17); the launches traced: 657 us -> 112 us
  local copies, waits for them, and re-layouts: 240 us -> 11 us
  other arithmetic: 153 us -> 0.7 us
  waiting for transfers between devices: 103 us -> 0 us
  Pallas kernels: 0 us -> 97.3 us
  blocking collectives: 70.7 us -> 0 us
  matrix products: 39.5 us -> 0 us
  starting transfers between devices: 26.9 us -> 0 us
  between operations: 23.3 us -> 3.29 us
    pallas_call x0 -> x2, Pallas kernels: none -> 97.3 us  [the longest x1 70.1 us: per_device(): pl.pallas_call(functools.partial(local_kernel, nf, npat), out_shape=(jax....]
    scatter-add x1 -> x0, other arithmetic: 95 us -> none  [spread(): jnp.zeros((count, 4 * width), jnp.float32).at[slot_ids[0]].add(terms)]
    gather x2 -> x0, local copies, waits for them, and re-layouts: 82.5 us -> none  [interpolate(): picked = jnp.take(table, slot_ids[0], axis=0).reshape(-1, 4, width)]
    psum x1 -> x0, waiting for transfers between devices: 70.9 us -> none  [per_device(): lax.psum((up_grad, mix_grad, head_grad), ('face', 'patch'))]
    psum x1 -> x0, blocking collectives: 70.7 us -> none  [per_device(): lax.psum((up_grad, mix_grad, head_grad), ('face', 'patch'))]
    dot_general x48 -> x0, matrix products: 39.5 us -> none  [the longest x27 12.4 us: matmul_taps(): result = jnp.dot(weight, flat, preferred_element_type=jnp.float32)]
    slice x20 -> x2, local copies, waits for them, and re-layouts: 41.1 us -> 2.67 us  [the longest x1 1.48 us: per_device(): coarse[:, :, 0]]
    ppermute x16 -> x0, waiting for transfers between devices: 32.5 us -> none  [the longest x4 18.1 us: extended_2(): lax.ppermute(lax.slice_in_dim(block, block.shape[dim] - width, None, axis...]
  transfers between devices with their start and end apart: 17 -> 0, of which waited for: 9 -> 0; matrix products, arithmetic and copies ran while one was open for 28% -> 0% of each run, Pallas kernels for 0% -> 0%
where the time goes in v1:
time: 113 us; the launch traced here: 112 us
  Pallas kernels  97.3 us (86%)
  local copies, waits for them, and re-layouts  11 us (10%)
  between operations  3.29 us (3%)
    pallas_call x1, Pallas kernels, per_device(): pl.pallas_call(functools.partial(local_kernel, nf, npat), out_shape=(jax....  70.1 us
    pallas_call x1, Pallas kernels, per_device(): pl.pallas_call(functools.partial(sum_kernel, nf, npat), out_shape=(jax.Sh...  27.3 us
    unnamed x20, local copies, waits for them, and re-layouts  7.19 us

profile of v1, /device:TPU:1, one launch (start us, length us, event | category | flops | bytes accessed | tf_op | source)
XLA Modules:
  0.0 112.3 jit_solution(15283574166759845244)
XLA Ops:
  0.6 1.2 %slice.9 = s32[1,1,1]{2,1,0:T(1,128)} slice(s32[1,4,4096]{2,1,0:T(4,128)} %param.12), slice={[0:1], [2:3], [0:1]} | slice | bytes 8 | tf_op jit(solution)/shard_map/slice | solution.py:481
  4.4 1.5 %fusion = (bf16[128,16,1]{2,1,0:T(8,128)(2,1)S(1)}, bf16[128,16,1]{2,1,0:T(8,128)(2,1)S(1)}) fusion(bf16[128,16,128]{2,1,0:T(8,128)(2,1)} %param.8), kind=kLoop, calls=%fused_computation.2 | loop fusion | bytes 16384 | tf_op jit(solution)/shard_map/slice | solution.py:477
  5.9 0.8 copy.24
  6.8 0.0 copy-start.4
  6.8 0.8 copy.25
  7.6 0.0 copy-start.1
  7.6 0.1 pad.2.clone
  7.7 0.7 maximum_maximum_fusion.edge_ref
  8.4 0.0 copy-done.4
  8.4 0.1 copy.21
  8.5 0.2 reshape.21.wmix_ref
  8.7 0.0 copy-start.2
  8.7 0.7 copy.22
  9.4 0.0 copy-done.2
  9.4 0.0 copy-done.1
  9.5 0.0 copy-start.5
  9.5 0.9 copy.27
  10.4 0.0 copy-done.5
  10.4 0.7 copy.23
  11.1 70.1 %local.1 = (f32[8,16384]{1,0:T(8,128)}, f32[1024,128]{1,0:T(8,128)}) custom-call(s32[1]{0:T(128)S(6)} %select_n.5.start_ref, bf16[16,128,128]{2,1,0:T(8,128)(2,1)} %bitcast.13, bf16[128,128]{1,0:T(8,128)(2,1)} %maximum_maximum_fusion.edge_ref, bf16[3,3,64,128]{3,2,1,0:T(8,128)(2,1)} %wup_ref.1, bf16[192,192]{1,0:T(8,128)(2,1)} %copy-done.2, ...), custom_call_target="tpu_custom_call" | custom-call | tf_op jit(solution)/shard_map/local/pallas_call | solution.py:509
  81.2 0.0 copy-start
  81.2 1.0 copy-done
  82.2 0.0 copy-start.3
  82.2 27.3 %sum.1 = (f32[576,128]{1,0:T(8,128)S(1)}, f32[576,64]{1,0:T(8,128)S(1)}, f32[8,64]{1,0:T(8,128)S(1)}) custom-call(f32[1024,128]{1,0:T(8,128)S(1)} %copy-done), custom_call_target="tpu_custom_call" | custom-call | tf_op jit(solution)/shard_map/sum/pallas_call | solution.py:530
  109.5 0.0 copy-done.3
  109.5 0.8 copy.32
  110.3 0.7 copy.33
  111.0 0.7 copy.34
  111.7 0.6 copy.35
  (1 shorter events, 0.0 us)
Async XLA Ops:
  6.8 1.6 %copy-start.4 = (bf16[3,3,64,64]{3,2,1,0:T(8,128)(2,1)S(1)}, bf16[3,3,64,64]{3,2,1,0:T(8,128)(2,1)}, u32[]{:S(2)}) copy-start(bf16[3,3,64,64]{3,2,1,0:T(8,128)(2,1)} %param.10) | copy-start | bytes 221188
  7.6 1.8 %copy-start.1 = (bf16[128,16,128]{2,1,0:T(8,128)(2,1)S(1)}, bf16[128,16,128]{2,1,0:T(8,128)(2,1)}, u32[]{:S(2)}) copy-start(bf16[128,16,128]{2,1,0:T(8,128)(2,1)} %param.8) | copy-start | bytes 1572868
  8.7 0.8 copy-start.2
  9.5 0.9 copy-start.5
  81.2 1.0 copy-start
  82.2 27.3 %copy-start.3 = (f32[8,16384]{1,0:T(8,128)S(1)}, f32[8,16384]{1,0:T(8,128)}, u32[]{:S(2)}) copy-start(f32[8,16384]{1,0:T(8,128)} %get-tuple-element.20) | copy-start | bytes 1572868

commit v2 on v1

--- a/solution.py
+++ b/solution.py
@@ -16,7 +16,7 @@
 CF = 64
 COUT = 8
 COLS = 16
-POINT_TILE = 512
+POINT_TILE = 2048
 GRAD_ROWS = 1024
 MIX_ROW = 9 * CF
 HEAD_ROW = MIX_ROW + 6 * CF
@@ -46,20 +46,22 @@
 
 def row_weights(slot, along):
     width = slot.shape[1]
+    larger = jnp.maximum(along, 1.0 - along)
+    upper, lower = along / larger, (1.0 - along) / larger
     place = lax.broadcasted_iota(jnp.int32, (256, width), 0)
     natural = 2 * (place & 127) + (place >> 7)
     away = natural - (slot & 255)
-    weight = jnp.where(away == 0, 1.0 - along, jnp.where(away == 1, along, 0.0))
-    return weight.astype(BF16)
+    weight = jnp.where(away == 0, lower, jnp.where(away == 1, upper, 0.0))
+    return weight.astype(BF16), larger
 
 
 def local_kernel(
     nf, npat,
-    start_ref, coarse_ref, edge_ref, wup_ref, wmix_ref, wback_ref, whead_ref, wheadt_ref,
+    send_ref, coarse_ref, wup_ref, wmix_ref, whead_ref,
     slot_ref, frac_ref, cot_ref,
     head_ref, grad_ref,
-    ext, exts, edges, upw, hid, slope1, slope2, feat, gown, gsend, table,
-    sacc, srecv, pad, sc, strip, strips, zbuf, fc, mixacc, upacc,
+    ext, exts, edges, upw, mixw, backw, hid, slope1, slope2, feat, gown, gsend, table,
+    sacc, srecv, pad, sc, strip, strips, zbuf, mixacc, upacc, starts, start_sem,
     send_sem, recv_sem,
 ):
     me_f, me_p = lax.axis_index("face"), lax.axis_index("patch")
@@ -67,6 +69,8 @@
     def device(df, dp):
         return (lax.rem(me_f + df + nf, nf), lax.rem(me_p + dp + npat, npat))
 
+    start_copy = pltpu.make_async_copy(send_ref.at[0, :, pl.ds(0, LANES)], starts, start_sem)
+    start_copy.start()
     barrier = pltpu.get_barrier_semaphore()
     partners = NEIGHBOURS + ((0, 2), (0, -2))
     for df, dp in partners:
@@ -86,12 +90,21 @@
         copies.append(copy)
         return copy
 
+    lane = lax.broadcasted_iota(jnp.int32, (CIN, LANES), 1)
+    lane64 = lane[:CF]
+    edge = jnp.zeros((CIN, LANES), F32)
+    for j in range(COLS):
+        column = coarse_ref[j].astype(F32)
+        edge = jnp.where(lane == j, turn(column, j), edge)
+        edge = jnp.where(lane == COLS + j, turn(column, COLS + 1 + j), edge)
+    edge_own = edges.at[len(NEIGHBOURS)]
+    edge_own[...] = edge.astype(BF16)
     coarse_copies = [
         send(coarse_ref.at[0], ext.at[COLS + 1], (0, -1)),
         send(coarse_ref.at[COLS - 1], ext.at[0], (0, 1)),
     ]
     for number, offset in enumerate(NEIGHBOURS):
-        coarse_copies.append(send(edge_ref, edges.at[number], offset))
+        coarse_copies.append(send(edge_own, edges.at[number], offset))
 
     ext[1 : COLS + 1] = coarse_ref[...]
     ext[COLS + 2] = jnp.zeros((CIN, LANES), BF16)
@@ -102,6 +115,13 @@
         upw[low, CIN:] = jnp.zeros((CF, CIN), BF16)
         upw[high, :CIN] = wup_ref[2, row_tap]
         upw[high, CIN:] = wup_ref[0, row_tap]
+    mix_rows = [
+        jnp.concatenate([wmix_ref[col_tap, row_tap].astype(F32) for col_tap in range(3)], axis=1)
+        for row_tap in range(3)
+    ]
+    mixing = jnp.concatenate(mix_rows, axis=0)
+    mixw[...] = mixing.astype(BF16)
+    backw[...] = mixing.T.astype(BF16)
 
     sacc[...] = jnp.zeros_like(sacc)
 
@@ -110,8 +130,8 @@
         here = pl.ds(pl.multiple_of(step * POINT_TILE, POINT_TILE), POINT_TILE)
         slot = slot_ref[0:1, here]
         along, across = frac_ref[0:1, here], frac_ref[1:2, here]
-        rows = row_weights(slot, along)
-        cot = cot_ref[:, here]
+        rows, larger = row_weights(slot, along)
+        cot = cot_ref[:, here] * larger
         near, far = cot * (1.0 - across), cot * across
         column = jnp.broadcast_to(slot >> 8, near.shape)[None]
         number = lax.broadcasted_iota(jnp.int32, (64,) + near.shape, 0)
@@ -131,8 +151,6 @@
 
     for copy in coarse_copies:
         copy.wait_recv()
-    lane = lax.broadcasted_iota(jnp.int32, (CIN, LANES), 1)
-    lane64 = lane[:CF]
     above = jnp.where(me_f > 0, 1.0, 0.0).astype(F32)
     below = jnp.where(me_f < nf - 1, 1.0, 0.0).astype(F32)
 
@@ -146,7 +164,7 @@
     top = jnp.where(between(1, 17, lane), turn(arrived(edges, -1, 0), -15), 0.0)
     top = jnp.where(lane == 0, turn(arrived(edges, -1, -1), -31), top)
     top = jnp.where(lane == 17, turn(arrived(edges, -1, 1), 1), top) * above
-    first_row = jnp.where(between(33, 49, lane), turn(edge_ref[...].astype(F32), 33), 0.0)
+    first_row = jnp.where(between(33, 49, lane), turn(edge, 33), 0.0)
     first_row = jnp.where(lane == 32, turn(arrived(edges, 0, -1), 17), first_row)
     first_row = jnp.where(lane == 49, turn(arrived(edges, 0, 1), 49), first_row)
     bottom = jnp.where(between(65, 81, lane), turn(arrived(edges, 1, 0), 65), 0.0)
@@ -163,11 +181,11 @@
         rim_hidden.append(value * sigmoid(value))
     even_rim, odd_rim = rim_hidden
     mix_rim = [
-        dot(wmix_ref[...], jnp.concatenate([turn(odd_rim, 1), even_rim, odd_rim], axis=0).astype(BF16)),
-        dot(wmix_ref[...], jnp.concatenate([even_rim, odd_rim, turn(even_rim, -1)], axis=0).astype(BF16)),
-    ]
-
-    @pl.loop(0, 9)
+        dot(mixw[...], jnp.concatenate([turn(odd_rim, 1), even_rim, odd_rim], axis=0).astype(BF16)),
+        dot(mixw[...], jnp.concatenate([even_rim, odd_rim, turn(even_rim, -1)], axis=0).astype(BF16)),
+    ]
+
+    @pl.loop(0, 9, unroll=9)
     def _(step):
         t = 2 * step
         pair = [ext[pl.ds(t + k, 2)].reshape(2 * CIN, LANES) for k in range(2)]
@@ -193,7 +211,7 @@
         values = []
         for parity in range(2):
             q = 2 * j + parity
-            out = dot(wmix_ref[...], hid[pl.ds(q + 1, 3)].reshape(192, 256))
+            out = dot(mixw[...], hid[pl.ds(q + 1, 3)].reshape(192, 256))
             low, mid, high = out[0:64], out[64:128], out[128:192]
             first = turn(mix_rim[parity][0:64], 127 - j)
             last = turn(mix_rim[parity][128:192], 62 - j)
@@ -210,22 +228,23 @@
             values.append(point_value)
         gsend[j] = jnp.concatenate(values, axis=0).astype(BF16)
 
-    pl.loop(0, 8)(mix_step)
+    pl.loop(0, 8, unroll=8)(mix_step)
     value_copies = [
         send(gsend.at[0:8], table.at[0:8], (0, -2)),
         send(gsend.at[0:8], table.at[8:16], (0, -1)),
     ]
-    pl.loop(8, 16)(mix_step)
+    pl.loop(8, 16, unroll=8)(mix_step)
     value_copies.append(send(gsend.at[8:16], table.at[24:32], (0, 1)))
 
-    start = start_ref[0]
+    start_copy.wait()
+    start = starts[2, 0] // 256
     for k in range(8):
         pair = [gown[start + 2 * k], gown[start + 2 * k + 1]]
         table[16 + k] = jnp.concatenate(pair, axis=0).astype(BF16)
 
     for copy in back_copies:
         copy.wait_recv()
-    weight_t = wheadt_ref[...]
+    weight_t = whead_ref[...].T
     high_t = weight_t.astype(BF16).astype(F32)
     weight_three = jnp.concatenate([high_t, weight_t - high_t, high_t], axis=1).astype(BF16)
     strip[...] = jnp.zeros_like(strip)
@@ -252,8 +271,8 @@
         total = row_of(2, q - 16) + pad[16 + q - start]
         return cot_step(q, total, head_sum)
 
-    head_sum = lax.fori_loop(0, 16, cot_low, jnp.zeros((COUT, CF), F32))
-    head_sum = lax.fori_loop(16, 32, cot_high, head_sum)
+    head_sum = lax.fori_loop(0, 16, cot_low, jnp.zeros((COUT, CF), F32), unroll=8)
+    head_sum = lax.fori_loop(16, 32, cot_high, head_sum, unroll=8)
     strips_own = strips.at[len(ROW_NEIGHBOURS)]
     strips_own[...] = strip[...].astype(BF16)
     cot_copies = [
@@ -271,13 +290,13 @@
         here = pl.ds(pl.multiple_of(step * POINT_TILE, POINT_TILE), POINT_TILE)
         slot = slot_ref[0:1, here]
         along, across = frac_ref[0:1, here], frac_ref[1:2, here]
-        rows = row_weights(slot, along)
+        rows, larger = row_weights(slot, along)
         columns = dot(table[...].reshape(64 * COUT, 256), rows).reshape(64, COUT, POINT_TILE)
         column = jnp.broadcast_to(slot >> 8, (COUT, POINT_TILE))[None]
         number = lax.broadcasted_iota(jnp.int32, (64, COUT, POINT_TILE), 0)
         away = number - column
-        near = jnp.broadcast_to(1.0 - across, (COUT, POINT_TILE))[None]
-        far = jnp.broadcast_to(across, (COUT, POINT_TILE))[None]
+        near = jnp.broadcast_to((1.0 - across) * larger, (COUT, POINT_TILE))[None]
+        far = jnp.broadcast_to(across * larger, (COUT, POINT_TILE))[None]
         weights = jnp.where(away == 0, near, jnp.where(away == 1, far, 0.0))
         head_ref[:, here] = jnp.sum(weights * columns, axis=0)
 
@@ -300,13 +319,13 @@
             [jnp.concatenate([odd, last], axis=1), value, jnp.concatenate([first, even], axis=1)],
             axis=0,
         ).astype(BF16)
-        zbuf[w] = dot(wback_ref[...], taps)
+        zbuf[w] = dot(backw[...], taps)
         return taps
 
     mixacc[...] = jnp.zeros_like(mixacc)
     back_step(0)
 
-    @pl.loop(1, 33)
+    @pl.loop(1, 33, unroll=8)
     def _(w):
         taps = back_step(w)
         mixacc[...] += dot_nt(taps, hid[pl.ds(w, 3)].reshape(192, 256))
@@ -315,7 +334,7 @@
 
     upacc[...] = jnp.zeros_like(upacc)
 
-    @pl.loop(0, 8)
+    @pl.loop(0, 8, unroll=8)
     def _(step):
         evens, odds = [], []
         for k in range(2):
@@ -473,19 +492,15 @@
 
 def per_device(nf, npat, coarse, w_up, w_mix, w_head, send_index, slot_ids, fractions, head_cot):
     by_column = coarse.transpose(1, 0, 2)
-    edge = jnp.concatenate(
-        [coarse[:, :, 0], coarse[:, :, -1], jnp.zeros((CIN, LANES - 2 * COLS), BF16)], axis=1
-    )
-    mixing = w_mix.transpose(1, 2, 0, 3).reshape(3 * CF, 3 * CF)
-    back = mixing.T
-    start = send_index[0, 2, 0:1] // 256
     points = slot_ids.shape[1]
     run = COLS * COUT
     scratch = [
         pltpu.VMEM((COLS + 3, CIN, LANES), BF16),
         pltpu.VMEM((COLS + 2, CIN, LANES), BF16),
-        pltpu.VMEM((len(NEIGHBOURS), CIN, LANES), BF16),
+        pltpu.VMEM((len(NEIGHBOURS) + 1, CIN, LANES), BF16),
         pltpu.VMEM((6 * CF, 2 * CIN), BF16),
+        pltpu.VMEM((3 * CF, 3 * CF), BF16),
+        pltpu.VMEM((3 * CF, 3 * CF), BF16),
         pltpu.VMEM((36, CF, 256), BF16),
         pltpu.VMEM((36, CF, 256), F32),
         pltpu.VMEM((32, CF, 256), F32),
@@ -500,9 +515,10 @@
         pltpu.VMEM((CF, LANES), F32),
         pltpu.VMEM((len(ROW_NEIGHBOURS) + 1, CF, LANES), BF16),
         pltpu.VMEM((34, 3 * CF, 256), F32),
-        pltpu.VMEM((8, LANES), F32),
         pltpu.VMEM((3 * CF, 3 * CF), F32),
         pltpu.VMEM((3, 2 * CF, 2 * CIN), F32),
+        pltpu.SMEM((4, LANES), jnp.int32),
+        pltpu.SemaphoreType.DMA,
         pltpu.SemaphoreType.DMA((24,)),
         pltpu.SemaphoreType.DMA((24,)),
     ]
@@ -512,14 +528,14 @@
             jax.ShapeDtypeStruct((COUT, points), F32),
             jax.ShapeDtypeStruct((GRAD_ROWS, LANES), F32),
         ),
-        in_specs=[pl.BlockSpec(memory_space=pltpu.SMEM)] + vmem(10),
+        in_specs=[pl.BlockSpec(memory_space=pl.ANY)] + vmem(7),
         out_specs=tuple(vmem(2)),
         scratch_shapes=scratch,
         compiler_params=pltpu.CompilerParams(
             collective_id=0, has_side_effects=True, vmem_limit_bytes=56 * 2**20
         ),
         name="local",
-    )(start, by_column, edge, w_up, mixing, back, w_head, w_head.T, slot_ids, fractions, head_cot)
+    )(send_index, by_column, w_up, w_mix, w_head, slot_ids, fractions, head_cot)
 
     nz, nx = stages_of(nf, npat)
     nzy = nz * nf

time: 113 us -> 82.2 us (0.73)
  Pallas kernels: 97.3 us -> 75.5 us
  local copies, waits for them, and re-layouts: 11 us -> 5.83 us
  between operations: 3.29 us -> 0.66 us
    pallas_call x1, Pallas kernels: 70.1 us -> 49.4 us  [per_device(): pl.pallas_call(functools.partial(local_kernel, nf, npat), out_shape=(jax....]
    slice x2 -> x0, local copies, waits for them, and re-layouts: 2.67 us -> none  [the longest x1 1.48 us: per_device(): coarse[:, :, 0]]
    unnamed x20 -> x9, local copies, waits for them, and re-layouts: 7.19 us -> 5.83 us
    pallas_call x1, Pallas kernels: 27.3 us -> 26.1 us  [per_device(): pl.pallas_call(functools.partial(sum_kernel, nf, npat), out_shape=(jax.Sh...]
where the time goes in v2:
time: 82.2 us; the launch traced here: 82 us
  Pallas kernels  75.5 us (92%)
  local copies, waits for them, and re-layouts  5.83 us (7%)
    pallas_call x1, Pallas kernels, per_device(): pl.pallas_call(functools.partial(local_kernel, nf, npat), out_shape=(jax....  49.4 us
    pallas_call x1, Pallas kernels, per_device(): pl.pallas_call(functools.partial(sum_kernel, nf, npat), out_shape=(jax.Sh...  26.1 us
    unnamed x9, local copies, waits for them, and re-layouts  5.83 us

profile of v2, /device:TPU:1, one launch (start us, length us, event | category | flops | bytes accessed | tf_op | source)
XLA Modules:
  0.0 82.0 jit_solution(4922503270890539762)
XLA Ops:
  0.6 2.0 %copy.14 = bf16[128,16,128]{2,0,1:T(8,128)(2,1)} copy(bf16[128,16,128]{2,1,0:T(8,128)(2,1)} %param.8) | data formatting | bytes 1048576 | tf_op args[0]
  2.6 49.4 %local.1 = (f32[8,16384]{1,0:T(8,128)}, f32[1024,128]{1,0:T(8,128)}) custom-call(s32[1,4,4096]{2,1,0:T(4,128)} %send_ref.1, bf16[16,128,128]{2,1,0:T(8,128)(2,1)} %bitcast.7, bf16[3,3,64,128]{3,2,1,0:T(8,128)(2,1)} %wup_ref.1, bf16[3,3,64,64]{3,2,1,0:T(8,128)(2,1)} %wmix_ref.1, f32[8,64]{1,0:T(8,128)} %whead_ref.1, s32[4,16384]{1,0:T(4,128)} %slot_ref.1, ...), custom_call_target="tpu_custom_call" | custom-call | tf_op jit(solution)/shard_map/local/pallas_call | solution.py:525
  52.0 0.0 copy-start
  52.0 1.0 %copy-done = f32[1024,128]{1,0:T(8,128)S(1)} copy-done((f32[1024,128]{1,0:T(8,128)S(1)}, f32[1024,128]{1,0:T(8,128)}, u32[]{:S(2)}) %copy-start) | copy-done | bytes 524312
  53.0 0.0 copy-start.1
  53.0 26.1 %sum.1 = (f32[576,128]{1,0:T(8,128)S(1)}, f32[576,64]{1,0:T(8,128)S(1)}, f32[8,64]{1,0:T(8,128)S(1)}) custom-call(f32[1024,128]{1,0:T(8,128)S(1)} %copy-done), custom_call_target="tpu_custom_call" | custom-call | tf_op jit(solution)/shard_map/sum/pallas_call | solution.py:546
  79.1 0.0 copy-done.1
  79.1 0.8 copy.19
  79.9 0.7 copy.20
  80.7 0.7 copy.21
  81.4 0.6 copy.22
Async XLA Ops:
  52.0 1.0 %copy-start = (f32[1024,128]{1,0:T(8,128)S(1)}, f32[1024,128]{1,0:T(8,128)}, u32[]{:S(2)}) copy-start(f32[1024,128]{1,0:T(8,128)} %get-tuple-element.10.grad_ref) | copy-start | bytes 1572868
  53.0 26.1 %copy-start.1 = (f32[8,16384]{1,0:T(8,128)S(1)}, f32[8,16384]{1,0:T(8,128)}, u32[]{:S(2)}) copy-start(f32[8,16384]{1,0:T(8,128)} %get-tuple-element.18) | copy-start | bytes 1572868

commit v3 on v2

--- a/solution.py
+++ b/solution.py
@@ -17,6 +17,7 @@
 COUT = 8
 COLS = 16
 POINT_TILE = 2048
+SAMPLE_CUTS = (3, 5, 7)
 GRAD_ROWS = 1024
 MIX_ROW = 9 * CF
 HEAD_ROW = MIX_ROW + 6 * CF
@@ -59,9 +60,10 @@
     nf, npat,
     send_ref, coarse_ref, wup_ref, wmix_ref, whead_ref,
     slot_ref, frac_ref, cot_ref,
-    head_ref, grad_ref,
+    head_ref, up_ref, mix_ref, headg_ref,
     ext, exts, edges, upw, mixw, backw, hid, slope1, slope2, feat, gown, gsend, table,
     sacc, srecv, pad, sc, strip, strips, zbuf, mixacc, upacc, starts, start_sem,
+    grads, final, total, other, parts, sum_send, sum_recv,
     send_sem, recv_sem,
 ):
     me_f, me_p = lax.axis_index("face"), lax.axis_index("patch")
@@ -73,9 +75,25 @@
     start_copy.start()
     barrier = pltpu.get_barrier_semaphore()
     partners = NEIGHBOURS + ((0, 2), (0, -2))
+    chips = nf * npat // 2
+    core = lax.rem(me_p, 2)
+    here_chip = me_f * (npat // 2) + me_p // 2
+    core_peer = (me_f, me_p + 1 - 2 * core)
+
+    def chip_at(k):
+        face = lax.rem(me_f + k // (npat // 2), nf)
+        pair = lax.rem(me_p // 2 + k % (npat // 2), npat // 2)
+        return face * (npat // 2) + pair, (face, 2 * pair + core)
+
     for df, dp in partners:
         pl.semaphore_signal(barrier, inc=1, device_id=device(df, dp), device_id_type=MESH)
-    pl.semaphore_wait(barrier, len(partners))
+    pl.semaphore_signal(barrier, inc=1, device_id=core_peer, device_id_type=MESH)
+
+    @pl.loop(1, chips)
+    def _(k):
+        pl.semaphore_signal(barrier, inc=1, device_id=chip_at(k)[1], device_id_type=MESH)
+
+    pl.semaphore_wait(barrier, len(partners) + chips)
 
     copies = []
 
@@ -285,8 +303,7 @@
     for copy in value_copies:
         copy.wait_recv()
 
-    @pl.loop(0, slot_ref.shape[1] // POINT_TILE)
-    def _(step):
+    def sample(step):
         here = pl.ds(pl.multiple_of(step * POINT_TILE, POINT_TILE), POINT_TILE)
         slot = slot_ref[0:1, here]
         along, across = frac_ref[0:1, here], frac_ref[1:2, here]
@@ -299,6 +316,16 @@
         far = jnp.broadcast_to(across * larger, (COUT, POINT_TILE))[None]
         weights = jnp.where(away == 0, near, jnp.where(away == 1, far, 0.0))
         head_ref[:, here] = jnp.sum(weights * columns, axis=0)
+
+    tiles = slot_ref.shape[1] // POINT_TILE
+    cuts = [0] + [tiles * part // 8 for part in SAMPLE_CUTS] + [tiles]
+    segments = iter(zip(cuts[:-1], cuts[1:]))
+
+    def sample_next():
+        first, last = next(segments)
+        pl.loop(first, last)(sample)
+
+    sample_next()
 
     for copy in cot_copies:
         copy.wait_recv()
@@ -362,117 +389,58 @@
     for row_tap in range(3):
         for col_tap, rows, lanes in ((0, 64, 128), (1, 0, 0), (2, 64, 0)):
             at = (col_tap * 3 + row_tap) * CF
-            grad_ref[at : at + CF] = upacc[row_tap, rows : rows + CF, lanes : lanes + LANES]
-    grad_ref[MIX_ROW : MIX_ROW + 192] = mixacc[:, :LANES]
-    grad_ref[MIX_ROW + 192 : HEAD_ROW] = jnp.concatenate(
+            grads[at : at + CF] = upacc[row_tap, rows : rows + CF, lanes : lanes + LANES]
+    grads[MIX_ROW : MIX_ROW + 192] = mixacc[:, :LANES]
+    grads[MIX_ROW + 192 : HEAD_ROW] = jnp.concatenate(
         [mixacc[:, LANES:], jnp.zeros((192, CF), F32)], axis=1
     )
-    grad_ref[HEAD_ROW : HEAD_ROW + COUT] = jnp.concatenate(
+    grads[HEAD_ROW : HEAD_ROW + COUT] = jnp.concatenate(
         [head_sum, jnp.zeros((COUT, CF), F32)], axis=1
     )
-    grad_ref[HEAD_ROW + COUT :] = jnp.zeros((GRAD_ROWS - HEAD_ROW - COUT, LANES), F32)
-    for copy in copies:
-        copy.wait_send()
-
-
-def stages_of(nf, npat):
-    nz = min(4, max(1, npat // 2))
-    nx = npat // (2 * nz)
-    return nz, nx
-
-
-def sum_kernel(nf, npat, grad_ref, up_ref, mix_ref, headg_ref, total, final, one, two, three, send_sem, recv_sem):
-    nz, nx = stages_of(nf, npat)
-    me_f, me_p = lax.axis_index("face"), lax.axis_index("patch")
-    core = lax.rem(me_p, 2)
-    z = lax.rem(me_p // 2, nz)
-    x = me_p // (2 * nz)
-
-    def core_peer(k):
-        return (me_f, me_p - core + lax.rem(core + k, 2))
-
-    def x_peer(k):
-        return (me_f, lax.rem(x + k, nx) * 2 * nz + z * 2 + core)
-
-    def zy_peer(k):
-        kz, kf = k % nz, k // nz
-        return (lax.rem(me_f + kf, nf), x * 2 * nz + lax.rem(z + kz, nz) * 2 + core)
-
-    nzy = nz * nf
+    grads[HEAD_ROW + COUT :] = jnp.zeros((GRAD_ROWS - HEAD_ROW - COUT, LANES), F32)
+
     half = GRAD_ROWS // 2
-    quarter = half // nx
-    piece = quarter // nzy
-    groups = ((core_peer, 2), (x_peer, nx), (zy_peer, nzy))
-
-    barrier = pltpu.get_barrier_semaphore()
-    count = 0
-    for peer, size in groups:
-        for k in range(1, size):
-            pl.semaphore_signal(barrier, inc=1, device_id=peer(k), device_id_type=MESH)
-            count += 1
-    pl.semaphore_wait(barrier, count)
-
-    sems = [0]
-    pending = []
-
-    def send(source, target, device):
-        number = sems[0]
-        sems[0] += 1
-        copy = pltpu.make_async_remote_copy(
-            src_ref=source, dst_ref=target,
-            send_sem=send_sem.at[number], recv_sem=recv_sem.at[number],
-            device_id=device, device_id_type=MESH,
-        )
-        copy.start()
-        pending.append(copy)
-        return copy
+    piece = half // chips
 
     def rows(start, size):
         return pl.ds(pl.multiple_of(start, 8), size)
 
-    def index_core(k):
-        return lax.rem(core + k, 2)
-
-    def index_x(k):
-        return lax.rem(x + k, nx)
-
-    def index_zy(k):
-        return lax.rem(me_f + k // nz, nf) * nz + lax.rem(z + k % nz, nz)
-
-    copy = send(grad_ref.at[rows(index_core(1) * half, half)], one.at[0], core_peer(1))
-    copy.wait_recv()
-    base = index_core(0) * half
-    total[rows(base, half)] = grad_ref[rows(base, half)] + one[0]
-    arrivals = [
-        send(total.at[rows(base + index_x(k) * quarter, quarter)], two.at[k - 1], x_peer(k))
-        for k in range(1, nx)
-    ]
-    base_x = base + index_x(0) * quarter
-    value = total[rows(base_x, quarter)]
-    for k, copy in enumerate(arrivals):
-        copy.wait_recv()
-        value = value + two[k]
-    total[rows(base_x, quarter)] = value
-    arrivals = [
-        send(total.at[rows(base_x + index_zy(k) * piece, piece)], three.at[k - 1], zy_peer(k))
-        for k in range(1, nzy)
-    ]
-    base_zy = base_x + index_zy(0) * piece
-    value = total[rows(base_zy, piece)]
-    for k, copy in enumerate(arrivals):
-        copy.wait_recv()
-        value = value + three[k]
-    final[rows(base_zy, piece)] = value
-
-    def share(start, size, peer, count):
-        region = final.at[rows(start, size)]
-        started = [send(region, region, peer(k)) for k in range(1, count)]
-        for copy in started:
-            copy.wait_recv()
-
-    share(base_zy, piece, zy_peer, nzy)
-    share(base_x, quarter, x_peer, nx)
-    share(base, half, core_peer, 2)
+    def part(number, source, target, peer):
+        return pltpu.make_async_remote_copy(
+            src_ref=source, dst_ref=target,
+            send_sem=sum_send.at[number], recv_sem=sum_recv.at[number],
+            device_id=peer, device_id_type=MESH,
+        )
+
+    base = core * half
+    own = rows(here_chip * piece, piece)
+    own_final = final.at[rows(base + here_chip * piece, piece)]
+
+    def spread_part(k):
+        number, peer = chip_at(k)
+        return part(k, total.at[rows(number * piece, piece)], parts.at[k - 1], peer)
+
+    def share_part(k):
+        return part(chips + k, own_final, own_final, chip_at(k)[1])
+
+    first = part(0, grads.at[rows((1 - core) * half, half)], other, core_peer)
+    first.start()
+    sample_next()
+    first.wait_recv()
+    total[...] = grads[rows(base, half)] + other[...]
+
+    pl.loop(1, chips)(lambda k: spread_part(k).start())
+    sample_next()
+    pl.loop(1, chips)(lambda k: spread_part(k).wait_recv())
+    final[rows(base + here_chip * piece, piece)] = total[own] + jnp.sum(parts[...], axis=0)
+
+    pl.loop(1, chips)(lambda k: share_part(k).start())
+    sample_next()
+    pl.loop(1, chips)(lambda k: share_part(k).wait_recv())
+    half_final = final.at[rows(base, half)]
+    last = part(chips, half_final, half_final, core_peer)
+    last.start()
+    last.wait_recv()
 
     up_ref[...] = final[:MIX_ROW]
     for col_tap in range(3):
@@ -482,7 +450,15 @@
             to = (col_tap * 3 + row_tap) * CF
             mix_ref[to : to + CF] = final[at : at + CF, lanes : lanes + CF]
     headg_ref[...] = final[HEAD_ROW : HEAD_ROW + COUT, :CF]
-    for copy in pending:
+    first.wait_send()
+    last.wait_send()
+
+    @pl.loop(1, chips)
+    def _(k):
+        spread_part(k).wait_send()
+        share_part(k).wait_send()
+
+    for copy in copies:
         copy.wait_send()
 
 
@@ -494,6 +470,7 @@
     by_column = coarse.transpose(1, 0, 2)
     points = slot_ids.shape[1]
     run = COLS * COUT
+    chips, half = nf * npat // 2, GRAD_ROWS // 2
     scratch = [
         pltpu.VMEM((COLS + 3, CIN, LANES), BF16),
         pltpu.VMEM((COLS + 2, CIN, LANES), BF16),
@@ -519,17 +496,26 @@
         pltpu.VMEM((3, 2 * CF, 2 * CIN), F32),
         pltpu.SMEM((4, LANES), jnp.int32),
         pltpu.SemaphoreType.DMA,
+        pltpu.VMEM((GRAD_ROWS, LANES), F32),
+        pltpu.VMEM((GRAD_ROWS, LANES), F32),
+        pltpu.VMEM((half, LANES), F32),
+        pltpu.VMEM((half, LANES), F32),
+        pltpu.VMEM((chips - 1, half // chips, LANES), F32),
+        pltpu.SemaphoreType.DMA((2 * chips,)),
+        pltpu.SemaphoreType.DMA((2 * chips,)),
         pltpu.SemaphoreType.DMA((24,)),
         pltpu.SemaphoreType.DMA((24,)),
     ]
-    head, grads = pl.pallas_call(
+    head, up, mix, head_grad = pl.pallas_call(
         functools.partial(local_kernel, nf, npat),
         out_shape=(
             jax.ShapeDtypeStruct((COUT, points), F32),
-            jax.ShapeDtypeStruct((GRAD_ROWS, LANES), F32),
+            jax.ShapeDtypeStruct((9 * CF, CIN), F32),
+            jax.ShapeDtypeStruct((9 * CF, CF), F32),
+            jax.ShapeDtypeStruct((COUT, CF), F32),
         ),
         in_specs=[pl.BlockSpec(memory_space=pl.ANY)] + vmem(7),
-        out_specs=tuple(vmem(2)),
+        out_specs=tuple(vmem(4)),
         scratch_shapes=scratch,
         compiler_params=pltpu.CompilerParams(
             collective_id=0, has_side_effects=True, vmem_limit_bytes=56 * 2**20
@@ -537,35 +523,6 @@
         name="local",
     )(send_index, by_column, w_up, w_mix, w_head, slot_ids, fractions, head_cot)
 
-    nz, nx = stages_of(nf, npat)
-    nzy = nz * nf
-    half = GRAD_ROWS // 2
-    quarter = half // nx
-    piece = quarter // nzy
-    sends = 2 * (1 + nx - 1 + nzy - 1)
-    up, mix, head_grad = pl.pallas_call(
-        functools.partial(sum_kernel, nf, npat),
-        out_shape=(
-            jax.ShapeDtypeStruct((9 * CF, CIN), F32),
-            jax.ShapeDtypeStruct((9 * CF, CF), F32),
-            jax.ShapeDtypeStruct((COUT, CF), F32),
-        ),
-        in_specs=vmem(1),
-        out_specs=tuple(vmem(3)),
-        scratch_shapes=[
-            pltpu.VMEM((GRAD_ROWS, LANES), F32),
-            pltpu.VMEM((GRAD_ROWS, LANES), F32),
-            pltpu.VMEM((1, half, LANES), F32),
-            pltpu.VMEM((max(1, nx - 1), quarter, LANES), F32),
-            pltpu.VMEM((nzy - 1, piece, LANES), F32),
-            pltpu.SemaphoreType.DMA((sends,)),
-            pltpu.SemaphoreType.DMA((sends,)),
-        ],
-        compiler_params=pltpu.CompilerParams(
-            collective_id=1, has_side_effects=True, vmem_limit_bytes=32 * 2**20
-        ),
-        name="sum",
-    )(grads)
     return head, up.reshape(3, 3, CF, CIN), mix.reshape(3, 3, CF, CF), head_grad
 
 

time: 82.2 us -> 73.6 us (0.90)
  Pallas kernels: 75.5 us -> 66.4 us
    pallas_call x1 -> x0, Pallas kernels: 26.1 us -> none  [per_device(): pl.pallas_call(functools.partial(sum_kernel, nf, npat), out_shape=(jax.Sh...]
    pallas_call x1, Pallas kernels: 49.4 us -> 66.4 us  [per_device(): pl.pallas_call(functools.partial(local_kernel, nf, npat), out_shape=(jax....]
    unnamed x9 -> x11, local copies, waits for them, and re-layouts: 5.83 us -> 6.27 us
where the time goes in v3:
time: 73.6 us; the launch traced here: 73.4 us
  Pallas kernels  66.4 us (90%)
  local copies, waits for them, and re-layouts  6.27 us (9%)
    pallas_call x1, Pallas kernels, per_device(): pl.pallas_call(functools.partial(local_kernel, nf, npat), out_shape=(jax....  66.4 us
    unnamed x11, local copies, waits for them, and re-layouts  6.27 us

profile of v3, /device:TPU:1, one launch (start us, length us, event | category | flops | bytes accessed | tf_op | source)
XLA Modules:
  0.0 73.4 jit_solution(5263943323223406200)
XLA Ops:
  0.6 2.0 %copy.14 = bf16[128,16,128]{2,0,1:T(8,128)(2,1)} copy(bf16[128,16,128]{2,1,0:T(8,128)(2,1)} %param.8) | data formatting | bytes 1048576 | tf_op args[0]
  2.6 66.4 %local.1 = (f32[8,16384]{1,0:T(8,128)}, f32[576,128]{1,0:T(8,128)}, f32[576,64]{1,0:T(8,128)}, f32[8,64]{1,0:T(8,128)}) custom-call(s32[1,4,4096]{2,1,0:T(4,128)} %send_ref.1, bf16[16,128,128]{2,1,0:T(8,128)(2,1)} %bitcast.5, bf16[3,3,64,128]{3,2,1,0:T(8,128)(2,1)} %wup_ref.1, bf16[3,3,64,64]{3,2,1,0:T(8,128)(2,1)} %wmix_ref.1, f32[8,64]{1,0:T(8,128)} %whead_ref.1, ...), custom_call_target="tpu_custom_call" | custom-call | tf_op jit(solution)/shard_map/local/pallas_call | solution.py:509
  69.0 0.0 copy-start.1
  69.1 1.9 %copy.19 = f32[8,16384]{1,0:T(8,128)} copy(f32[8,16384]{1,0:T(8,128)} %get-tuple-element.16) | data formatting | bytes 1048576
  71.0 0.0 copy-done.1
  71.0 0.0 copy-start
  71.0 0.7 copy.20
  71.7 0.4 copy-done
  72.0 0.0 copy-start.2
  72.0 0.7 copy.21
  72.8 0.0 copy-done.2
  72.8 0.6 copy.22
Async XLA Ops:
  69.0 1.9 %copy-start.1 = (f32[576,128]{1,0:T(8,128)S(1)}, f32[576,128]{1,0:T(8,128)}, u32[]{:S(2)}) copy-start(f32[576,128]{1,0:T(8,128)} %get-tuple-element.9) | copy-start | bytes 884740
  71.0 1.1 %copy-start = (f32[576,64]{1,0:T(8,128)S(1)}, f32[576,64]{1,0:T(8,128)}, u32[]{:S(2)}) copy-start(f32[576,64]{1,0:T(8,128)} %get-tuple-element.10) | copy-start | bytes 442372
  72.0 0.7 copy-start.2

commit v4 on v3

--- a/solution.py
+++ b/solution.py
@@ -110,21 +110,21 @@
 
     lane = lax.broadcasted_iota(jnp.int32, (CIN, LANES), 1)
     lane64 = lane[:CF]
+    ext[1 : COLS + 1] = jnp.swapaxes(coarse_ref[...], 0, 1)
     edge = jnp.zeros((CIN, LANES), F32)
     for j in range(COLS):
-        column = coarse_ref[j].astype(F32)
+        column = ext[j + 1].astype(F32)
         edge = jnp.where(lane == j, turn(column, j), edge)
         edge = jnp.where(lane == COLS + j, turn(column, COLS + 1 + j), edge)
     edge_own = edges.at[len(NEIGHBOURS)]
     edge_own[...] = edge.astype(BF16)
     coarse_copies = [
-        send(coarse_ref.at[0], ext.at[COLS + 1], (0, -1)),
-        send(coarse_ref.at[COLS - 1], ext.at[0], (0, 1)),
+        send(ext.at[1], ext.at[COLS + 1], (0, -1)),
+        send(ext.at[COLS], ext.at[0], (0, 1)),
     ]
     for number, offset in enumerate(NEIGHBOURS):
         coarse_copies.append(send(edge_own, edges.at[number], offset))
 
-    ext[1 : COLS + 1] = coarse_ref[...]
     ext[COLS + 2] = jnp.zeros((CIN, LANES), BF16)
     for row_tap in range(3):
         low = slice(row_tap * CF, (row_tap + 1) * CF)
@@ -462,12 +462,17 @@
         copy.wait_send()
 
 
+def move_kernel(*refs):
+    count = len(refs) // 2
+    for k in range(count):
+        refs[count + k][...] = refs[k][...]
+
+
 def vmem(count):
     return [pl.BlockSpec(memory_space=pltpu.VMEM)] * count
 
 
 def per_device(nf, npat, coarse, w_up, w_mix, w_head, send_index, slot_ids, fractions, head_cot):
-    by_column = coarse.transpose(1, 0, 2)
     points = slot_ids.shape[1]
     run = COLS * COUT
     chips, half = nf * npat // 2, GRAD_ROWS // 2
@@ -521,8 +526,17 @@
             collective_id=0, has_side_effects=True, vmem_limit_bytes=56 * 2**20
         ),
         name="local",
-    )(send_index, by_column, w_up, w_mix, w_head, slot_ids, fractions, head_cot)
-
+    )(send_index, coarse, w_up, w_mix, w_head, slot_ids, fractions, head_cot)
+
+    results = (head, up, mix, head_grad)
+    head, up, mix, head_grad = pl.pallas_call(
+        move_kernel,
+        out_shape=tuple(jax.ShapeDtypeStruct(one.shape, one.dtype) for one in results),
+        in_specs=vmem(4),
+        out_specs=tuple(vmem(4)),
+        compiler_params=pltpu.CompilerParams(vmem_limit_bytes=56 * 2**20),
+        name="move",
+    )(*results)
     return head, up.reshape(3, 3, CF, CIN), mix.reshape(3, 3, CF, CF), head_grad
 
 

time: 73.6 us -> 69.5 us (0.944)
  local copies, waits for them, and re-layouts: 6.27 us -> 0 us
  Pallas kernels: 66.4 us -> 68.7 us
    unnamed x11 -> x0, local copies, waits for them, and re-layouts: 6.27 us -> none
    pallas_call x0 -> x1, Pallas kernels: none -> 2.22 us  [per_device(): pl.pallas_call(move_kernel, out_shape=tuple((jax.ShapeDtypeStruct(one.sha...]
where the time goes in v4:
time: 69.5 us; the launch traced here: 69.4 us
  Pallas kernels  68.7 us (99%)
    pallas_call x1, Pallas kernels, per_device(): pl.pallas_call(functools.partial(local_kernel, nf, npat), out_shape=(jax....  66.5 us
    pallas_call x1, Pallas kernels, per_device(): pl.pallas_call(move_kernel, out_shape=tuple((jax.ShapeDtypeStruct(one.sha...  2.22 us

profile of v4, /device:TPU:1, one launch (start us, length us, event | category | flops | bytes accessed | tf_op | source)
XLA Modules:
  0.0 69.4 jit_solution(5634269279172865063)
XLA Ops:
  0.6 66.5 %local.1 = (f32[8,16384]{1,0:T(8,128)}, f32[576,128]{1,0:T(8,128)}, f32[576,64]{1,0:T(8,128)}, f32[8,64]{1,0:T(8,128)}) custom-call(s32[1,4,4096]{2,1,0:T(4,128)} %send_ref.1, bf16[128,16,128]{2,1,0:T(8,128)(2,1)} %coarse_ref.1, bf16[3,3,64,128]{3,2,1,0:T(8,128)(2,1)} %wup_ref.1, bf16[3,3,64,64]{3,2,1,0:T(8,128)(2,1)} %wmix_ref.1, f32[8,64]{1,0:T(8,128)} %whead_ref.1, ...), custom_call_target="tpu_custom_call" | custom-call | tf_op jit(solution)/shard_map/local/pallas_call | solution.py:514
  67.1 2.2 %move.1 = (f32[8,16384]{1,0:T(8,128)}, f32[576,128]{1,0:T(8,128)}, f32[576,64]{1,0:T(8,128)}, f32[8,64]{1,0:T(8,128)}) custom-call(f32[8,16384]{1,0:T(8,128)} %get-tuple-element.12.refs_0_, f32[576,128]{1,0:T(8,128)} %get-tuple-element.13.refs_1_, f32[576,64]{1,0:T(8,128)} %get-tuple-element.14.refs_2_, f32[8,64]{1,0:T(8,128)} %get-tuple-element.15.refs_3_), custom_call_target="tpu_custom_call" | custom-call | tf_op jit(solution)/shard_map/move/pallas_call | solution.py:532

commit v5 on v4

--- a/solution.py
+++ b/solution.py
@@ -17,6 +17,7 @@
 COUT = 8
 COLS = 16
 POINT_TILE = 2048
+EARLY = 2
 SAMPLE_CUTS = (3, 5, 7)
 GRAD_ROWS = 1024
 MIX_ROW = 9 * CF
@@ -93,7 +94,6 @@
     def _(k):
         pl.semaphore_signal(barrier, inc=1, device_id=chip_at(k)[1], device_id_type=MESH)
 
-    pl.semaphore_wait(barrier, len(partners) + chips)
 
     copies = []
 
@@ -118,13 +118,6 @@
         edge = jnp.where(lane == COLS + j, turn(column, COLS + 1 + j), edge)
     edge_own = edges.at[len(NEIGHBOURS)]
     edge_own[...] = edge.astype(BF16)
-    coarse_copies = [
-        send(ext.at[1], ext.at[COLS + 1], (0, -1)),
-        send(ext.at[COLS], ext.at[0], (0, 1)),
-    ]
-    for number, offset in enumerate(NEIGHBOURS):
-        coarse_copies.append(send(edge_own, edges.at[number], offset))
-
     ext[COLS + 2] = jnp.zeros((CIN, LANES), BF16)
     for row_tap in range(3):
         low = slice(row_tap * CF, (row_tap + 1) * CF)
@@ -143,8 +136,7 @@
 
     sacc[...] = jnp.zeros_like(sacc)
 
-    @pl.loop(0, slot_ref.shape[1] // POINT_TILE)
-    def _(step):
+    def scatter(step):
         here = pl.ds(pl.multiple_of(step * POINT_TILE, POINT_TILE), POINT_TILE)
         slot = slot_ref[0:1, here]
         along, across = frac_ref[0:1, here], frac_ref[1:2, here]
@@ -156,6 +148,19 @@
         away = number - column
         terms = jnp.where(away == 0, near[None], jnp.where(away == 1, far[None], 0.0))
         sacc[...] += dot_nt(terms.reshape(64 * COUT, POINT_TILE).astype(BF16), rows)
+
+    tiles = slot_ref.shape[1] // POINT_TILE
+    early = tiles * EARLY // 8
+    pl.loop(0, early)(scatter)
+    pl.semaphore_wait(barrier, len(partners) + chips)
+    coarse_copies = [
+        send(ext.at[1], ext.at[COLS + 1], (0, -1)),
+        send(ext.at[COLS], ext.at[0], (0, 1)),
+    ]
+    for number, offset in enumerate(NEIGHBOURS):
+        coarse_copies.append(send(edge_own, edges.at[number], offset))
+
+    pl.loop(early, tiles)(scatter)
 
     run = COLS * COUT
     pad[0:16] = jnp.zeros((16, COUT, 256), F32)

time: 69.5 us -> 67.1 us (0.965)
  Pallas kernels: 68.7 us -> 66.2 us
    pallas_call x1, Pallas kernels: 66.5 us -> 64 us  [per_device(): pl.pallas_call(functools.partial(local_kernel, nf, npat), out_shape=(jax....]
where the time goes in v5:
time: 67.1 us; the launch traced here: 66.9 us
  Pallas kernels  66.2 us (99%)
    pallas_call x1, Pallas kernels, per_device(): pl.pallas_call(functools.partial(local_kernel, nf, npat), out_shape=(jax....  64 us
    pallas_call x1, Pallas kernels, per_device(): pl.pallas_call(move_kernel, out_shape=tuple((jax.ShapeDtypeStruct(one.sha...  2.22 us

profile of v5, /device:TPU:1, one launch (start us, length us, event | category | flops | bytes accessed | tf_op | source)
XLA Modules:
  0.0 66.9 jit_solution(6857069103108279192)
XLA Ops:
  0.6 64.0 %local.1 = (f32[8,16384]{1,0:T(8,128)}, f32[576,128]{1,0:T(8,128)}, f32[576,64]{1,0:T(8,128)}, f32[8,64]{1,0:T(8,128)}) custom-call(s32[1,4,4096]{2,1,0:T(4,128)} %send_ref.1, bf16[128,16,128]{2,1,0:T(8,128)(2,1)} %coarse_ref.1, bf16[3,3,64,128]{3,2,1,0:T(8,128)(2,1)} %wup_ref.1, bf16[3,3,64,64]{3,2,1,0:T(8,128)(2,1)} %wmix_ref.1, f32[8,64]{1,0:T(8,128)} %whead_ref.1, ...), custom_call_target="tpu_custom_call" | custom-call | tf_op jit(solution)/shard_map/local/pallas_call | solution.py:519
  64.7 2.2 %move.1 = (f32[8,16384]{1,0:T(8,128)}, f32[576,128]{1,0:T(8,128)}, f32[576,64]{1,0:T(8,128)}, f32[8,64]{1,0:T(8,128)}) custom-call(f32[8,16384]{1,0:T(8,128)} %get-tuple-element.12.refs_0_, f32[576,128]{1,0:T(8,128)} %get-tuple-element.13.refs_1_, f32[576,64]{1,0:T(8,128)} %get-tuple-element.14.refs_2_, f32[8,64]{1,0:T(8,128)} %get-tuple-element.15.refs_3_), custom_call_target="tpu_custom_call" | custom-call | tf_op jit(solution)/shard_map/move/pallas_call | solution.py:537

commit v6 on v5

--- a/solution.py
+++ b/solution.py
@@ -18,7 +18,7 @@
 COLS = 16
 POINT_TILE = 2048
 EARLY = 2
-SAMPLE_CUTS = (3, 5, 7)
+SAMPLE_CUTS = (2, 3, 6)
 GRAD_ROWS = 1024
 MIX_ROW = 9 * CF
 HEAD_ROW = MIX_ROW + 6 * CF

time: 67.1 us -> 65.5 us (0.976)
  Pallas kernels: 66.2 us -> 64.7 us
    pallas_call x1, Pallas kernels: 64 us -> 62.5 us  [per_device(): pl.pallas_call(functools.partial(local_kernel, nf, npat), out_shape=(jax....]
where the time goes in v6:
time: 65.5 us; the launch traced here: 65.4 us
  Pallas kernels  64.7 us (99%)
    pallas_call x1, Pallas kernels, per_device(): pl.pallas_call(functools.partial(local_kernel, nf, npat), out_shape=(jax....  62.5 us
    pallas_call x1, Pallas kernels, per_device(): pl.pallas_call(move_kernel, out_shape=tuple((jax.ShapeDtypeStruct(one.sha...  2.22 us

profile of v6, /device:TPU:1, one launch (start us, length us, event | category | flops | bytes accessed | tf_op | source)
XLA Modules:
  0.0 65.4 jit_solution(9306519948862738122)
XLA Ops:
  0.6 62.5 %local.1 = (f32[8,16384]{1,0:T(8,128)}, f32[576,128]{1,0:T(8,128)}, f32[576,64]{1,0:T(8,128)}, f32[8,64]{1,0:T(8,128)}) custom-call(s32[1,4,4096]{2,1,0:T(4,128)} %send_ref.1, bf16[128,16,128]{2,1,0:T(8,128)(2,1)} %coarse_ref.1, bf16[3,3,64,128]{3,2,1,0:T(8,128)(2,1)} %wup_ref.1, bf16[3,3,64,64]{3,2,1,0:T(8,128)(2,1)} %wmix_ref.1, f32[8,64]{1,0:T(8,128)} %whead_ref.1, ...), custom_call_target="tpu_custom_call" | custom-call | tf_op jit(solution)/shard_map/local/pallas_call | solution.py:519
  63.1 2.2 %move.1 = (f32[8,16384]{1,0:T(8,128)}, f32[576,128]{1,0:T(8,128)}, f32[576,64]{1,0:T(8,128)}, f32[8,64]{1,0:T(8,128)}) custom-call(f32[8,16384]{1,0:T(8,128)} %get-tuple-element.12.refs_0_, f32[576,128]{1,0:T(8,128)} %get-tuple-element.13.refs_1_, f32[576,64]{1,0:T(8,128)} %get-tuple-element.14.refs_2_, f32[8,64]{1,0:T(8,128)} %get-tuple-element.15.refs_3_), custom_call_target="tpu_custom_call" | custom-call | tf_op jit(solution)/shard_map/move/pallas_call | solution.py:537

commit v7 on v6

--- a/solution.py
+++ b/solution.py
@@ -22,8 +22,21 @@
 GRAD_ROWS = 1024
 MIX_ROW = 9 * CF
 HEAD_ROW = MIX_ROW + 6 * CF
+UP_HALF = MIX_ROW // 2
 NEIGHBOURS = tuple((df, dp) for df in (-1, 0, 1) for dp in (-1, 0, 1) if (df, dp) != (0, 0))
 ROW_NEIGHBOURS = tuple(pair for pair in NEIGHBOURS if pair[0] != 0)
+
+
+def placed_rows(start, size):
+    half = GRAD_ROWS // 2
+    middle = MIX_ROW + half - UP_HALF
+    runs = ((0, UP_HALF, 0), (UP_HALF, MIX_ROW, half), (MIX_ROW, middle, UP_HALF), (middle, GRAD_ROWS, half + UP_HALF))
+    found = []
+    for low, high, place in runs:
+        first, last = max(low, start), min(high, start + size)
+        if first < last:
+            found.append((first, last - first, place + first - low))
+    return found
 
 
 def dot(left, right):
@@ -364,6 +377,34 @@
 
     back_step(33)
 
+    half = GRAD_ROWS // 2
+    piece = half // chips
+
+    def rows(start, size):
+        return pl.ds(pl.multiple_of(start, 8), size)
+
+    def part(number, source, target, peer):
+        return pltpu.make_async_remote_copy(
+            src_ref=source, dst_ref=target,
+            send_sem=sum_send.at[number], recv_sem=sum_recv.at[number],
+            device_id=peer, device_id_type=MESH,
+        )
+
+    def half_part(number, start, size):
+        source = grads.at[rows((1 - core) * half + start, size)]
+        return part(number, source, other.at[start : start + size], core_peer)
+
+    def put(at, value):
+        for start, size, place in placed_rows(at, value.shape[0]):
+            grads[place : place + size] = value[start - at : start - at + size]
+
+    put(MIX_ROW, mixacc[:, :LANES])
+    put(MIX_ROW + 192, jnp.concatenate([mixacc[:, LANES:], jnp.zeros((192, CF), F32)], axis=1))
+    put(HEAD_ROW, jnp.concatenate([head_sum, jnp.zeros((COUT, CF), F32)], axis=1))
+    put(HEAD_ROW + COUT, jnp.zeros((GRAD_ROWS - HEAD_ROW - COUT, LANES), F32))
+    early_sum = half_part(0, UP_HALF, half - UP_HALF)
+    early_sum.start()
+
     upacc[...] = jnp.zeros_like(upacc)
 
     @pl.loop(0, 8, unroll=8)
@@ -392,30 +433,8 @@
         upacc[2] += dot_nt(odd, plain)
 
     for row_tap in range(3):
-        for col_tap, rows, lanes in ((0, 64, 128), (1, 0, 0), (2, 64, 0)):
-            at = (col_tap * 3 + row_tap) * CF
-            grads[at : at + CF] = upacc[row_tap, rows : rows + CF, lanes : lanes + LANES]
-    grads[MIX_ROW : MIX_ROW + 192] = mixacc[:, :LANES]
-    grads[MIX_ROW + 192 : HEAD_ROW] = jnp.concatenate(
-        [mixacc[:, LANES:], jnp.zeros((192, CF), F32)], axis=1
-    )
-    grads[HEAD_ROW : HEAD_ROW + COUT] = jnp.concatenate(
-        [head_sum, jnp.zeros((COUT, CF), F32)], axis=1
-    )
-    grads[HEAD_ROW + COUT :] = jnp.zeros((GRAD_ROWS - HEAD_ROW - COUT, LANES), F32)
-
-    half = GRAD_ROWS // 2
-    piece = half // chips
-
-    def rows(start, size):
-        return pl.ds(pl.multiple_of(start, 8), size)
-
-    def part(number, source, target, peer):
-        return pltpu.make_async_remote_copy(
-            src_ref=source, dst_ref=target,
-            send_sem=sum_send.at[number], recv_sem=sum_recv.at[number],
-            device_id=peer, device_id_type=MESH,
-        )
+        for col_tap, low, lanes in ((0, 64, 128), (1, 0, 0), (2, 64, 0)):
+            put((col_tap * 3 + row_tap) * CF, upacc[row_tap, low : low + CF, lanes : lanes + LANES])
 
     base = core * half
     own = rows(here_chip * piece, piece)
@@ -428,10 +447,11 @@
     def share_part(k):
         return part(chips + k, own_final, own_final, chip_at(k)[1])
 
-    first = part(0, grads.at[rows((1 - core) * half, half)], other, core_peer)
+    first = half_part(2 * chips, 0, UP_HALF)
     first.start()
     sample_next()
     first.wait_recv()
+    early_sum.wait_recv()
     total[...] = grads[rows(base, half)] + other[...]
 
     pl.loop(1, chips)(lambda k: spread_part(k).start())
@@ -447,15 +467,20 @@
     last.start()
     last.wait_recv()
 
-    up_ref[...] = final[:MIX_ROW]
+    for start, size, place in placed_rows(0, MIX_ROW):
+        up_ref[start : start + size] = final[place : place + size]
     for col_tap in range(3):
         for row_tap in range(3):
             at = MIX_ROW + (col_tap // 2) * 192 + row_tap * CF
             lanes = (col_tap % 2) * CF
             to = (col_tap * 3 + row_tap) * CF
-            mix_ref[to : to + CF] = final[at : at + CF, lanes : lanes + CF]
-    headg_ref[...] = final[HEAD_ROW : HEAD_ROW + COUT, :CF]
+            for start, size, place in placed_rows(at, CF):
+                here = to + start - at
+                mix_ref[here : here + size] = final[place : place + size, lanes : lanes + CF]
+    for start, size, place in placed_rows(HEAD_ROW, COUT):
+        headg_ref[start - HEAD_ROW : start - HEAD_ROW + size] = final[place : place + size, :CF]
     first.wait_send()
+    early_sum.wait_send()
     last.wait_send()
 
     @pl.loop(1, chips)
@@ -511,8 +536,8 @@
         pltpu.VMEM((half, LANES), F32),
         pltpu.VMEM((half, LANES), F32),
         pltpu.VMEM((chips - 1, half // chips, LANES), F32),
-        pltpu.SemaphoreType.DMA((2 * chips,)),
-        pltpu.SemaphoreType.DMA((2 * chips,)),
+        pltpu.SemaphoreType.DMA((2 * chips + 1,)),
+        pltpu.SemaphoreType.DMA((2 * chips + 1,)),
         pltpu.SemaphoreType.DMA((24,)),
         pltpu.SemaphoreType.DMA((24,)),
     ]

time: 65.5 us -> 65.7 us (level)
  no operation moved by 1% of the time
where the time goes in v7:
time: 65.7 us; the launch traced here: 65.5 us
  Pallas kernels  64.9 us (99%)
    pallas_call x1, Pallas kernels, per_device(): pl.pallas_call(functools.partial(local_kernel, nf, npat), out_shape=(jax....  62.7 us
    pallas_call x1, Pallas kernels, per_device(): pl.pallas_call(move_kernel, out_shape=tuple((jax.ShapeDtypeStruct(one.sha...  2.22 us

profile of v7, /device:TPU:1, one launch (start us, length us, event | category | flops | bytes accessed | tf_op | source)
XLA Modules:
  0.0 65.5 jit_solution(9374945000091037249)
XLA Ops:
  0.6 62.7 %local.1 = (f32[8,16384]{1,0:T(8,128)}, f32[576,128]{1,0:T(8,128)}, f32[576,64]{1,0:T(8,128)}, f32[8,64]{1,0:T(8,128)}) custom-call(s32[1,4,4096]{2,1,0:T(4,128)} %send_ref.1, bf16[128,16,128]{2,1,0:T(8,128)(2,1)} %coarse_ref.1, bf16[3,3,64,128]{3,2,1,0:T(8,128)(2,1)} %wup_ref.1, bf16[3,3,64,64]{3,2,1,0:T(8,128)(2,1)} %wmix_ref.1, f32[8,64]{1,0:T(8,128)} %whead_ref.1, ...), custom_call_target="tpu_custom_call" | custom-call | tf_op jit(solution)/shard_map/local/pallas_call | solution.py:544
  63.3 2.2 %move.1 = (f32[8,16384]{1,0:T(8,128)}, f32[576,128]{1,0:T(8,128)}, f32[576,64]{1,0:T(8,128)}, f32[8,64]{1,0:T(8,128)}) custom-call(f32[8,16384]{1,0:T(8,128)} %get-tuple-element.12.refs_0_, f32[576,128]{1,0:T(8,128)} %get-tuple-element.13.refs_1_, f32[576,64]{1,0:T(8,128)} %get-tuple-element.14.refs_2_, f32[8,64]{1,0:T(8,128)} %get-tuple-element.15.refs_3_), custom_call_target="tpu_custom_call" | custom-call | tf_op jit(solution)/shard_map/move/pallas_call | solution.py:562
